TPU v7x, 128 devices: a whole 4x4x4 slice. The times are simulated.
128 devices in a mesh: doc: 8 (over y, x_hi), cent: 16 (over z, x_lo, core).
Axes of the slice: x: 4 (x_hi: 2, x_lo: 2; x = x_hi * 2 + x_lo), y: 4, z: 4, core: 2. Of those that a mesh axis runs over, the one named last changes fastest.
Arguments:
- embeddings: float32 [65536, 1024], P(('doc', 'cent'))
- centroids: float32 [16384, 1024], P('cent')
- cluster: int32 [65536], P(('doc', 'cent')), may hold values from 0 to 16383, as said below
- slot: int32 [65536], P(('doc', 'cent')), may hold values from 0 to 7, as said below
Outputs:
- soft_cost: float32 [65536], P(('doc', 'cent'))
- dup_sim: float32 [65536], P(('doc', 'cent'))
Inputs may be any that keep to these rules, and one draw needn't show every extreme that they name: Owner device of row r is cluster[r] // 128; some owner device receives rows from every device. `slot`: slots of the rows of one device that have the same owner device are distinct; in every draw some owner device takes 8 rows from every device.
All inputs are finite; a program needn't handle non-finite values.
Results may differ from a plain program's by a relative error of at most 0.0003.
Values may be sent and summed in bfloat16 or wider, within the bound.
No kernel may reach another device: no remote copies, remote signals or barrier semaphores. Data moves between devices by JAX's collectives and lax.ppermute only.
A program may use at most 192 MiB of HBM per device.

v0:
```python
import jax
import jax.numpy as jnp
from jax import lax
from jax.sharding import PartitionSpec as P

inverse_temp = 256.0


def unit_rows(values):
    total = jnp.sum(values * values, axis=1, keepdims=True)
    return (values * lax.rsqrt(total + 1e-06)).astype(jnp.bfloat16)


def inner_rows(left, right):
    return lax.dot_general(
        left, right, (((1,), (1,)), ((), ())), preferred_element_type=jnp.float32
    )


def block_terms(part, centre):
    score = inner_rows(part, centre) * inverse_temp
    high = jnp.max(score, axis=1)
    return (high, jnp.sum(jnp.exp(score - high[:, None]), axis=1))


def join_terms(first, second):
    high = jnp.maximum(first[0], second[0])
    return (high, second[1] * jnp.exp(second[0] - high))


def owner_best(rows, ids):
    total = rows.shape[0]
    block = min(512, total)
    col_pos = jnp.arange(total)

    def one_block(index):
        start = index * block
        part = lax.dynamic_slice_in_dim(rows, start, block, 0)
        part_ids = lax.dynamic_slice_in_dim(ids, start, block, 0)
        gram = inner_rows(part, rows)
        row_pos = start + jnp.arange(block)
        mask = (
            (part_ids[:, None] == ids[None, :])
            & (ids[None, :] >= 0.0)
            & (col_pos[None, :] < row_pos[:, None])
        )
        return jnp.max(jnp.where(mask, gram, jnp.float32(-1.0)), axis=1)

    return lax.map(one_block, jnp.arange(total // block)).reshape(total)


def per_device(embeddings, centroids, cluster, slot):
    row_count, width = embeddings.shape
    doc_count = lax.axis_size("doc")
    cent_count = lax.axis_size("cent")
    devices = doc_count * cent_count
    per_owner = centroids.shape[0] // doc_count
    capacity = 2 * row_count // devices
    unit = unit_rows(embeddings)
    centre = unit_rows(centroids)
    start_terms = (jnp.full((row_count,), -1e30, jnp.float32), jnp.zeros((row_count,), jnp.float32))
    high, total = join_terms(
        start_terms, block_terms(unit, lax.all_gather(centre, "cent", axis=0, tiled=True))
    )
    soft_cost = 1.0 - (high + jnp.log(total)) / inverse_temp
    owner = cluster // per_owner
    local = (cluster % per_owner).astype(jnp.bfloat16)
    target = owner * capacity + slot
    send_rows = jnp.zeros((devices * capacity, width), jnp.bfloat16).at[target].set(unit)
    send_ids = jnp.full((devices * capacity,), -1.0, jnp.bfloat16).at[target].set(local)
    got_rows, got_ids = (
        lax.all_to_all(
            send_rows.reshape(devices, capacity, width),
            ("doc", "cent"),
            split_axis=0,
            concat_axis=0,
            tiled=True,
        ),
        lax.all_to_all(
            send_ids.reshape(devices, capacity),
            ("doc", "cent"),
            split_axis=0,
            concat_axis=0,
            tiled=True,
        ),
    )
    best = owner_best(
        got_rows.reshape(devices * capacity, width),
        got_ids.reshape(devices * capacity).astype(jnp.float32),
    )
    returned = lax.all_to_all(
        best.reshape(devices, capacity), ("doc", "cent"), split_axis=0, concat_axis=0, tiled=True
    )
    dup_sim = returned.reshape(devices * capacity)[target]
    return (soft_cost, dup_sim)


def solution(mesh):
    return jax.shard_map(
        per_device,
        mesh=mesh,
        in_specs=(
            P(("doc", "cent"), None),
            P("cent", None),
            P(("doc", "cent")),
            P(("doc", "cent")),
        ),
        out_specs=(P(("doc", "cent")), P(("doc", "cent"))),
        check_vma=False,
    )
```

profile of v0, /device:TPU:0, one launch (start us, length us, event | category | flops | bytes accessed | tf_op | source)
XLA Modules:
  0.0 259.6 jit_solution(17680688221776090694)
XLA Ops:
  7.2 0.0 all-gather.2.cloned.1.call-start
  7.2 0.0 copy-start
  7.2 2.7 %multiply_reduce_fusion.1 = f32[1024]{0:T(1024)S(1)} fusion(f32[1024,1024]{1,0:T(8,128)} %param.7), kind=kLoop, calls=%fused_computation.14 | loop fusion | flops 2096128 | bytes 4198400 | tf_op jit(solution)/shard_map/reduce_sum | solution.py:10
  9.9 0.7 copy-done
  10.7 0.0 copy-start.3
  10.7 1.6 multiply_convert_fusion
  12.3 0.0 copy-start.2
  12.3 0.0 copy-start.1
  12.3 0.0 all-gather.2.cloned.1.call-update
  12.3 0.0 copy-done.3
  12.3 0.6 copy-done.2
  13.0 3.8 %scatter_custom_fusion = bf16[1024]{0:T(1024)(128)(2,1)S(1)} fusion(s32[512]{0:T(512)S(1)} %get-tuple-element.58, bf16[512]{0:T(512)(128)(2,1)S(1)} %get-tuple-element.57, bf16[]{:T(256)} %constant.72.clone.1), kind=kCustom, calls=%fused_computation.42 | custom fusion | bytes 2050 | tf_op jit(solution)/shard_map/scatter | solution.py:70
  16.7 0.8 all_to_all.20
  17.5 11.1 %all-to-all-start = ((bf16[128,1,8]{2,1,0:T(2,128)(2,1)}), bf16[128,1,8]{2,1,0:T(2,128)(2,1)S(1)}, u32[]{:S(2)}, u32[]{:S(2)}) async-start(bf16[128,1,8]{2,1,0:T(2,128)(2,1)} %all_to_all.20), calls=%async_computation | async-start | bytes 131072 | tf_op jit(solution)/shard_map/all_to_all | solution.py:79
  28.6 0.0 copy-done.1
  28.7 0.2 multiply_reduce_fusion.2
  28.9 4.2 %scatter_custom_fusion.1 = bf16[1024,1024]{1,0:T(8,128)(2,1)} fusion(s32[512]{0:T(512)S(1)} %get-tuple-element.58, bf16[]{:T(256)} %constant.65.clone.1, f32[512,1024]{1,0:T(8,128)S(1)} %copy-done.1, f32[512]{0:T(512)S(1)} %add_rsqrt_fusion.1), kind=kCustom, calls=%fused_computation.17 | custom fusion | flops 1048576 | bytes 4196354 | tf_op jit(solution)/shard_map/scatter | solution.py:69
  33.1 5.1 %all-to-all-done = bf16[128,1,8]{2,1,0:T(2,128)(2,1)S(1)} async-done(((bf16[128,1,8]{2,1,0:T(2,128)(2,1)}), bf16[128,1,8]{2,1,0:T(2,128)(2,1)S(1)}, u32[]{:S(2)}, u32[]{:S(2)}) %all-to-all-start) | async-done | bytes 2080 | tf_op jit(solution)/shard_map/all_to_all | solution.py:79
  38.2 5.8 %all-to-all-start.1 = ((bf16[128,8,1024]{2,1,0:T(8,128)(2,1)}), bf16[128,8,1024]{2,1,0:T(8,128)(2,1)}, u32[]{:S(2)}, u32[]{:S(2)}) async-start(bf16[128,8,1024]{2,1,0:T(8,128)(2,1)} %bitcast.13), calls=%async_computation.1 | async-start | bytes 4194304 | tf_op jit(solution)/shard_map/all_to_all | solution.py:72
  44.0 0.2 convert_reduce_fusion
  44.2 0.1 reshape.54
  44.3 52.5 %all-to-all-done.1 = bf16[128,8,1024]{2,1,0:T(8,128)(2,1)} async-done(((bf16[128,8,1024]{2,1,0:T(8,128)(2,1)}), bf16[128,8,1024]{2,1,0:T(8,128)(2,1)}, u32[]{:S(2)}, u32[]{:S(2)}) %all-to-all-start.1) | async-done | bytes 2097184 | tf_op jit(solution)/shard_map/all_to_all | solution.py:72
  96.8 9.9 %while.11 = (s32[]{:T(128)}, f32[2,512]{1,0:T(2,128)S(1)}, s32[2]{0:T(128)S(1)}, f32[1024]{0:T(1024)S(1)}, bf16[1024,1024]{1,0:T(8,128)(2,1)}, /*index=5*/s32[]{:T(128)}, s32[1]{0:T(128)}, s32[]{:T(128)}, s32[]{:T(128)}) while((s32[]{:T(128)}, f32[2,512]{1,0:T(2,128)S(1)}, s32[2]{0:T(128)S(1)}, f32[1024]{0:T(1024)S(1)}, ...), condition=%wide.region_8.9_spmd.clone, body=%wide.region_6.8_spmd.clone.sunk | while | flops 1076888576 | bytes 3172527 | solution.py:49
  96.8 0.6 dynamic_slice.19
  98.0 0.1 dynamic_slice.20
  98.1 3.6 %select_reduce_fusion.2 = f32[512]{0:T(512)S(1)} fusion(bf16[1024,1024]{1,0:T(8,128)(2,1)} %get-tuple-element.114, s32[]{:T(128)S(6)} %select_n.45, s32[512]{0:T(512)S(1)} %iota_add_fusion.2, f32[1024]{0:T(1024)S(1)} %get-tuple-element.113, f32[512]{0:T(512)S(1)} %dynamic_slice.20, pred[1024]{0:T(1024)(128)(4,1)S(1)} %broadcast_compare_fusion.3), kind=kOutput, calls=%fused_computation.5.clone.1 | convolution fusion | flops 1076887040 | bytes 3156996 | tf_op jit(solution)/shard_map/while/body/eval_jaxpr/dot_general | solution.py:15
  101.7 0.6 dynamic_slice.19
  103.0 0.1 dynamic_slice.20
  103.1 3.6 %select_reduce_fusion.2 = f32[512]{0:T(512)S(1)} fusion(bf16[1024,1024]{1,0:T(8,128)(2,1)} %get-tuple-element.114, s32[]{:T(128)S(6)} %select_n.45, s32[512]{0:T(512)S(1)} %iota_add_fusion.2, f32[1024]{0:T(1024)S(1)} %get-tuple-element.113, f32[512]{0:T(512)S(1)} %dynamic_slice.20, pred[1024]{0:T(1024)(128)(4,1)S(1)} %broadcast_compare_fusion.3), kind=kOutput, calls=%fused_computation.5.clone.1 | convolution fusion | flops 1076887040 | bytes 3156996 | tf_op jit(solution)/shard_map/while/body/eval_jaxpr/dot_general | solution.py:15
  106.7 0.7 all_to_all.18
  107.4 4.7 %all-to-all-start.2 = ((f32[128,1,8]{2,1,0:T(1,128)}), f32[128,1,8]{2,1,0:T(1,128)S(1)}, u32[]{:S(2)}, u32[]{:S(2)}) async-start(f32[128,1,8]{2,1,0:T(1,128)} %bitcast.2), calls=%async_computation.2 | async-start | bytes 131072 | tf_op jit(solution)/shard_map/all_to_all | solution.py:91
  112.2 9.4 %all-to-all-done.2 = f32[128,1,8]{2,1,0:T(1,128)S(1)} async-done(((f32[128,1,8]{2,1,0:T(1,128)}), f32[128,1,8]{2,1,0:T(1,128)S(1)}, u32[]{:S(2)}, u32[]{:S(2)}) %all-to-all-start.2) | async-done | bytes 4128 | tf_op jit(solution)/shard_map/all_to_all | solution.py:91
  121.6 0.5 broadcast.69
  122.1 0.8 reduce.7
  122.9 0.1 reshape.53
  123.0 3.4 %gather_fusion = f32[512]{0:T(512)} fusion(f32[1024]{0:T(1024)S(1)} %reshape.53, s32[1024]{0:T(1024)S(1)} %pad_clamp_fusion), kind=kCustom, calls=%fused_computation | custom fusion | bytes 6144 | tf_op jit(solution)/shard_map/gather | solution.py:94
  126.4 83.0 %all-gather.2.cloned.1.call-done = bf16[16384,1024]{1,0:T(8,128)(2,1)} async-done(((bf16[1024,1024]{1,0:T(8,128)(2,1)}), bf16[16384,1024]{1,0:T(8,128)(2,1)}) %all-gather.2.cloned.1.call-update) | async-done | bytes 33554448 | tf_op jit(solution)/shard_map/all_gather | solution.py:63
  209.4 28.6 %multiply_reduce_fusion = (f32[512]{0:T(512)S(1)}, f32[512,16384]{1,0:T(8,128)}) fusion(bf16[16384,1024]{1,0:T(8,128)(2,1)} %all-gather.2.cloned.1.call-done, f32[512,1024]{1,0:T(8,128)S(1)} %copy-done.1, f32[512]{0:T(512)S(1)} %add_rsqrt_fusion.1), kind=kOutput, calls=%fused_computation.12 | convolution fusion | flops 17197694976 | bytes 69210112 | tf_op jit(solution)/shard_map/dot_general | solution.py:15
  238.1 14.1 %exponential_reduce_fusion = f32[512]{0:T(512)S(1)} fusion(f32[512,16384]{1,0:T(8,128)} %get-tuple-element.60, f32[512]{0:T(512)S(1)} %get-tuple-element.59), kind=kLoop, calls=%fused_computation.11 | loop fusion | flops 25165312 | bytes 33558528 | tf_op jit(solution)/shard_map/reduce_sum | solution.py:23
  252.1 0.6 fusion.11
  (12 shorter events, 0.1 us)
Async XLA Ops:
  7.2 202.3 %all-gather.2.cloned.1.call-start = ((), (), s32[]{:S(2)}) async-start(), calls=%async_computation.3 | async-start | bytes 35651584 | tf_op jit(solution)/shard_map/all_gather | solution.py:63
  7.2 3.5 %copy-start = (f32[1024,1024]{1,0:T(8,128)S(1)}, f32[1024,1024]{1,0:T(8,128)}, u32[]{:S(2)}) copy-start(f32[1024,1024]{1,0:T(8,128)} %param.7) | copy-start | bytes 12582916
  10.7 1.6 copy-start.3
  12.3 0.7 copy-start.2
  12.3 16.4 %copy-start.1 = (f32[512,1024]{1,0:T(8,128)S(1)}, f32[512,1024]{1,0:T(8,128)}, u32[]{:S(2)}) copy-start(f32[512,1024]{1,0:T(8,128)} %param.6) | copy-start | bytes 6291460
  17.5 20.7 %all-to-all-start = ((bf16[128,1,8]{2,1,0:T(2,128)(2,1)}), bf16[128,1,8]{2,1,0:T(2,128)(2,1)S(1)}, u32[]{:S(2)}, u32[]{:S(2)}) async-start(bf16[128,1,8]{2,1,0:T(2,128)(2,1)} %all_to_all.20), calls=%async_computation | async-start | bytes 131072 | tf_op jit(solution)/shard_map/all_to_all | solution.py:79
  38.2 58.5 %all-to-all-start.1 = ((bf16[128,8,1024]{2,1,0:T(8,128)(2,1)}), bf16[128,8,1024]{2,1,0:T(8,128)(2,1)}, u32[]{:S(2)}, u32[]{:S(2)}) async-start(bf16[128,8,1024]{2,1,0:T(8,128)(2,1)} %bitcast.13), calls=%async_computation.1 | async-start | bytes 4194304 | tf_op jit(solution)/shard_map/all_to_all | solution.py:72
  107.4 14.2 %all-to-all-start.2 = ((f32[128,1,8]{2,1,0:T(1,128)}), f32[128,1,8]{2,1,0:T(1,128)S(1)}, u32[]{:S(2)}, u32[]{:S(2)}) async-start(f32[128,1,8]{2,1,0:T(1,128)} %bitcast.2), calls=%async_computation.2 | async-start | bytes 131072 | tf_op jit(solution)/shard_map/all_to_all | solution.py:91
Sparse Core Ops, SparseCore 0:
  12.4 196.9 all-gather.1
where the time goes:
time: 261 us; the launch traced here: 260 us
  waiting for transfers between devices  150 us (57%)
  matrix products  35.8 us (14%)
  other arithmetic  24.4 us (9%)
  starting transfers between devices  21.7 us (8%)
  between operations  14.1 us (5%)
  local copies, waits for them, and re-layouts  12.2 us (5%)
    all_gather x1, waiting for transfers between devices, per_device(): lax.all_gather(centre, 'cent', axis=0, tiled=True)  83 us
    all_to_all x1, waiting for transfers between devices, per_device(): lax.all_to_all(send_rows.reshape(devices, capacity, width), ('doc', 'cent...  52.5 us
    dot_general x3, matrix products, inner_rows(): lax.dot_general(left, right, (((1,), (1,)), ((), ())), preferred_element_...  35.8 us
    reduce_sum x1, other arithmetic, block_terms(): return (high, jnp.sum(jnp.exp(score - high[:, None]), axis=1))  14.1 us
    all_to_all x1, starting transfers between devices, per_device(): lax.all_to_all(send_ids.reshape(devices, capacity), ('doc', 'cent'), spli...  11.1 us
    all_to_all x1, waiting for transfers between devices, per_device(): lax.all_to_all(best.reshape(devices, capacity), ('doc', 'cent'), split_ax...  9.42 us
    all_to_all x1, starting transfers between devices, per_device(): lax.all_to_all(send_rows.reshape(devices, capacity, width), ('doc', 'cent...  5.79 us
  transfers between devices with their start and end apart: 4, of which 4 were waited for; matrix products, arithmetic and copies ran while one was open for 8% of the time, Pallas kernels for 0%

commit v1 on v0

v1 whole, which is shorter than its diff:
```python
import functools
import math

import jax
import jax.numpy as jnp
from jax import lax
from jax.experimental import pallas as pl
from jax.experimental.pallas import tpu as pltpu
from jax.sharding import PartitionSpec as P

INVERSE_TEMP = 256.0
SCALE = INVERSE_TEMP / math.log(2.0)
BACK = math.log(2.0) / INVERSE_TEMP
NT = (((1,), (1,)), ((), ()))
ID_LANES = 128
VMEM = pl.BlockSpec(memory_space=pltpu.VMEM)
LIMIT = 48 * 1024 * 1024


def params():
    return pltpu.CompilerParams(vmem_limit_bytes=LIMIT)


def unit_of(values):
    total = jnp.sum(values * values, axis=1, keepdims=True)
    return (values * lax.rsqrt(total + 1e-06)).astype(jnp.bfloat16)


def target_row(cluster, slot, per_owner, cap):
    return (cluster // per_owner) * cap + slot


def rows_kernel(per_owner, cap, emb_ref, cluster_ref, slot_ref, low_ref, high_ref, send_ref):
    unit = unit_of(emb_ref[...])
    half = unit.shape[0] // 2
    low_ref[...] = unit[:half]
    high_ref[...] = unit[half:]
    cluster = cluster_ref[...]
    target = target_row(cluster, slot_ref[...], per_owner, cap)
    local = (cluster % per_owner + 1).astype(jnp.float32)
    ids = jnp.broadcast_to(local, (ID_LANES, local.shape[1])).astype(jnp.bfloat16)
    total = send_ref.shape[0]
    width = unit.shape[1]
    block = 256
    for start in range(0, total, block):
        place = start + lax.broadcasted_iota(jnp.int32, (block, unit.shape[0]), 0)
        hot = (place == target).astype(jnp.float32).astype(jnp.bfloat16)
        send_ref[start : start + block, :width] = lax.dot_general(
            hot, unit, (((1,), (0,)), ((), ())), preferred_element_type=jnp.float32
        ).astype(jnp.bfloat16)
        send_ref[start : start + block, width:] = (
            lax.dot_general(hot, ids, NT, preferred_element_type=jnp.float32) - 1.0
        ).astype(jnp.bfloat16)


def prepare_rows(embeddings, cluster, slot, per_owner, cap, devices):
    rows, width = embeddings.shape
    half = jax.ShapeDtypeStruct((rows // 2, width), jnp.bfloat16)
    return pl.pallas_call(
        functools.partial(rows_kernel, per_owner, cap),
        out_shape=(
            half,
            half,
            jax.ShapeDtypeStruct((devices * cap, width + ID_LANES), jnp.bfloat16),
        ),
        in_specs=[VMEM] * 3,
        out_specs=(VMEM,) * 3,
        compiler_params=params(),
        cost_estimate=pl.CostEstimate(
            flops=2 * devices * cap * rows * width, bytes_accessed=6 * rows * width, transcendentals=0
        ),
        name="prepare_rows",
    )(embeddings, cluster.reshape(1, rows), slot.reshape(1, rows))


def centre_kernel(cen_ref, low_ref, high_ref):
    @pl.when(pl.program_id(0) < 2)
    def _():
        low_ref[...] = unit_of(cen_ref[...])

    @pl.when(pl.program_id(0) >= 2)
    def _():
        high_ref[...] = unit_of(cen_ref[...])


def prepare_centres(centroids):
    count, width = centroids.shape
    half = jax.ShapeDtypeStruct((count // 2, width), jnp.bfloat16)
    block = count // 4
    return pl.pallas_call(
        centre_kernel,
        grid=(4,),
        out_shape=(half, half),
        in_specs=[pl.BlockSpec((block, width), lambda i: (i, 0))],
        out_specs=(
            pl.BlockSpec((block, width), lambda i: (jnp.minimum(i, 1), 0)),
            pl.BlockSpec((block, width), lambda i: (jnp.maximum(i - 2, 0), 0)),
        ),
        compiler_params=params(),
        cost_estimate=pl.CostEstimate(
            flops=4 * count * width, bytes_accessed=6 * count * width, transcendentals=count
        ),
        name="prepare_centres",
    )(centroids)


def score_kernel(n_rows, n_cent, step, *refs):
    row_refs = refs[:n_rows]
    cent_refs = refs[n_rows : n_rows + n_cent]
    out_ref = refs[n_rows + n_cent]
    table, high, total, sems = refs[n_rows + n_cent + 1 :]
    part = cent_refs[0].shape[0]
    block = row_refs[0].shape[0]
    copies = [
        pltpu.make_async_copy(ref, table.at[pl.ds(i * part, part)], sems.at[i])
        for i, ref in enumerate(cent_refs)
    ]
    for copy in copies:
        copy.start()
    high[...] = jnp.full_like(high, -1e30)
    total[...] = jnp.zeros_like(total)
    for i in range(n_cent):
        copies[i].wait()

        @pl.loop(0, part // step)
        def _(k):
            start = pl.multiple_of(i * part + k * step, step)
            centre = table[pl.ds(start, step), :]
            for j in range(n_rows):
                lanes = slice(j * block, (j + 1) * block)
                score = SCALE * lax.dot_general(
                    centre, row_refs[j][...], NT, preferred_element_type=jnp.float32
                )
                score = score.reshape(step // 8, 8, block)
                before = high[:, lanes]
                now = jnp.maximum(before, jnp.max(score, axis=0))
                high[:, lanes] = now
                total[:, lanes] = total[:, lanes] * jnp.exp2(before - now) + jnp.sum(
                    jnp.exp2(score - now[None]), axis=0
                )

    top = jnp.max(high[...], axis=0, keepdims=True)
    all_sum = jnp.sum(total[...] * jnp.exp2(high[...] - top), axis=0, keepdims=True)
    out_ref[...] = top + jnp.log2(all_sum)


def score(rows, centres, name):
    block, width = rows[0].shape
    part = centres[0].shape[0]
    count = len(rows) * block
    table = len(centres) * part
    return pl.pallas_call(
        functools.partial(score_kernel, len(rows), len(centres), 256),
        out_shape=jax.ShapeDtypeStruct((1, count), jnp.float32),
        in_specs=[VMEM] * len(rows) + [pl.BlockSpec(memory_space=pl.ANY)] * len(centres),
        out_specs=VMEM,
        scratch_shapes=[
            pltpu.VMEM((table, width), jnp.bfloat16),
            pltpu.VMEM((8, count), jnp.float32),
            pltpu.VMEM((8, count), jnp.float32),
            pltpu.SemaphoreType.DMA((len(centres),)),
        ],
        compiler_params=params(),
        cost_estimate=pl.CostEstimate(
            flops=2 * count * table * width,
            bytes_accessed=2 * (count + table) * width,
            transcendentals=count * table,
        ),
        name=name,
    )(*rows, *centres)


def owner_kernel(rows_ref, out_ref):
    total = rows_ref.shape[0]
    width = rows_ref.shape[1] - ID_LANES
    block = 256
    pick = (lax.broadcasted_iota(jnp.int32, (8, ID_LANES), 1) == 0).astype(jnp.float32)
    pick = pick.astype(jnp.bfloat16)
    ids = rows_ref[:, width:]
    id_row = lax.dot_general(pick, ids, NT, preferred_element_type=jnp.float32)[:1]
    for col in range(0, total, block):
        best = jnp.full((8, block), -1.0, jnp.float32)
        for row in range(0, col + block, block):
            gram = lax.dot_general(
                rows_ref[row : row + block, :width],
                rows_ref[col : col + block, :width],
                NT,
                preferred_element_type=jnp.float32,
            )
            id_col = ids[row : row + block].astype(jnp.float32)
            id_col = jnp.concatenate([id_col] * (block // ID_LANES), axis=1)
            same = id_col == id_row[:, col : col + block]
            if row == col:
                s = lax.broadcasted_iota(jnp.int32, (block, block), 0)
                r = lax.broadcasted_iota(jnp.int32, (block, block), 1)
                same = same & (s < r)
            gram = jnp.where(same, gram, -1.0).reshape(block // 8, 8, block)
            best = jnp.maximum(best, jnp.max(gram, axis=0))
        out_ref[:, col : col + block] = jnp.max(best, axis=0, keepdims=True)


def owner_best(rows):
    total, width = rows.shape
    return pl.pallas_call(
        owner_kernel,
        out_shape=jax.ShapeDtypeStruct((1, total), jnp.float32),
        in_specs=[VMEM],
        out_specs=VMEM,
        compiler_params=params(),
        cost_estimate=pl.CostEstimate(
            flops=2 * total * total * width, bytes_accessed=2 * total * width, transcendentals=0
        ),
        name="owner_best",
    )(rows)


def pick_kernel(per_owner, got_ref, cluster_ref, slot_ref, out_ref):
    got = got_ref[...]
    devices, cap = got.shape
    rows = out_ref.shape[1]
    owner = cluster_ref[...] // per_owner
    hot = (lax.broadcasted_iota(jnp.int32, (devices, rows), 0) == owner).astype(jnp.float32)
    by_slot = lax.dot_general(
        got,
        hot,
        (((0,), (0,)), ((), ())),
        precision=lax.Precision.HIGHEST,
        preferred_element_type=jnp.float32,
    )
    mine = lax.broadcasted_iota(jnp.int32, (cap, rows), 0) == slot_ref[...]
    out_ref[...] = jnp.sum(jnp.where(mine, by_slot, 0.0), axis=0, keepdims=True)


def pick(got, cluster, slot, per_owner):
    rows = cluster.shape[0]
    return pl.pallas_call(
        functools.partial(pick_kernel, per_owner),
        out_shape=jax.ShapeDtypeStruct((1, rows), jnp.float32),
        in_specs=[VMEM] * 3,
        out_specs=VMEM,
        compiler_params=params(),
        cost_estimate=pl.CostEstimate(
            flops=16 * got.shape[0] * rows, bytes_accessed=32 * rows, transcendentals=0
        ),
        name="pick",
    )(got, cluster.reshape(1, rows), slot.reshape(1, rows)).reshape(rows)


def moves(step):
    pairs = []
    for y in range(4):
        for x in range(4):
            for z in range(4):
                for core in range(2):
                    here, there = [
                        (b * 2 + a // 2) * 16 + (c * 2 + a % 2) * 2 + d
                        for a, b, c, d in ((x, y, z, core), step(x, y, z, core))
                    ]
                    pairs.append((here, there))
    return pairs


def move_x(value, by):
    return lax.ppermute(
        value, ("doc", "cent"), moves(lambda x, y, z, core: ((x + by) % 4, y, z, core))
    )


def move_z(value, by):
    return lax.ppermute(value, ("doc", "cent"), moves(lambda x, y, z, core: (x, y, (z + by) % 4, core)))


def swap_core(value):
    return lax.ppermute(value, ("doc", "cent"), moves(lambda x, y, z, core: (x, y, z, 1 - core)))


def per_device(embeddings, centroids, cluster, slot):
    row_count, width = embeddings.shape
    devices = lax.axis_size("doc") * lax.axis_size("cent")
    per_owner = centroids.shape[0] // lax.axis_size("doc")
    cap = 2 * row_count // devices

    low, high, send = prepare_rows(embeddings, cluster, slot, per_owner, cap, devices)
    low_up, high_down = move_z(low, 1), move_z(high, -1)
    high_up, low_down = move_z(high, 1), move_z(low, -1)
    low_far, high_far = move_z(low_up, 1), move_z(high_down, -1)

    got = lax.all_to_all(
        send.reshape(devices, cap, width + ID_LANES),
        ("doc", "cent"),
        split_axis=0,
        concat_axis=0,
        tiled=True,
    )

    centre_low, centre_high = prepare_centres(centroids)
    side_low, side_high = move_x(centre_low, 1), move_x(centre_high, -1)
    core_low, core_high = swap_core(centre_low), swap_core(centre_high)
    side_core_low, side_core_high = swap_core(side_low), swap_core(side_high)
    centres = (
        centre_low,
        centre_high,
        core_low,
        core_high,
        side_low,
        side_high,
        side_core_low,
        side_core_high,
    )

    near = score((low, high, low_up, high_up, low_down, high_down), centres, "score_near")
    mine, below, above = [near[:, i * row_count : (i + 1) * row_count] for i in range(3)]
    far = score((low_far, high_far), centres, "score_far")

    best = owner_best(got.reshape(devices * cap, width + ID_LANES))
    returned = lax.all_to_all(
        best.reshape(devices, cap), ("doc", "cent"), split_axis=0, concat_axis=0, tiled=True
    )
    dup_sim = pick(returned, cluster, slot, per_owner)

    terms = jnp.concatenate([mine, move_z(below, -1), move_z(above, 1), move_z(far, 2)], axis=0)
    top = jnp.max(terms, axis=0)
    soft_cost = 1.0 - BACK * (top + jnp.log2(jnp.sum(jnp.exp2(terms - top[None]), axis=0)))
    return (soft_cost, dup_sim)


def solution(mesh):
    return jax.shard_map(
        per_device,
        mesh=mesh,
        in_specs=(
            P(("doc", "cent"), None),
            P("cent", None),
            P(("doc", "cent")),
            P(("doc", "cent")),
        ),
        out_specs=(P(("doc", "cent")), P(("doc", "cent"))),
        check_vma=False,
    )
```

time: 261 us -> 148 us (0.57)
  waiting for transfers between devices: 150 us -> 64.1 us
  Pallas kernels: 0 us -> 40.2 us
  matrix products: 35.8 us -> 0 us
  other arithmetic: 24.4 us -> 1.29 us
  between operations: 14.1 us -> 0.77 us
  starting transfers between devices: 21.7 us -> 33.2 us
  local copies, waits for them, and re-layouts: 12.2 us -> 7.01 us
    all_gather x1 -> x0, waiting for transfers between devices: 83 us -> none  [per_device(): lax.all_gather(centre, 'cent', axis=0, tiled=True)]
    all_to_all x3 -> x2, waiting for transfers between devices: 67 us -> 8.78 us  [the longest x1 8.78 us: per_device(): lax.all_to_all(best.reshape(devices, cap), ('doc', 'cent'), split_axis=0,...]
    ppermute x0 -> x15, waiting for transfers between devices: none -> 55.4 us  [the longest x9 53 us: move_z(): lax.ppermute(value, ('doc', 'cent'), moves(lambda x, y, z, core: (x, y, (...]
    pallas_call x0 -> x6, Pallas kernels: none -> 40.2 us  [the longest x2 30.3 us: score(): pl.pallas_call(functools.partial(score_kernel, len(rows), len(centres), 2...]
    dot_general x3 -> x0, matrix products: 35.8 us -> none  [inner_rows(): lax.dot_general(left, right, (((1,), (1,)), ((), ())), preferred_element_...]
    ppermute x0 -> x15, starting transfers between devices: none -> 17.5 us  [the longest x9 13.6 us: move_z(): lax.ppermute(value, ('doc', 'cent'), moves(lambda x, y, z, core: (x, y, (...]
    reduce_sum x3 -> x1, other arithmetic: 17 us -> 0.04 us  [per_device(): jnp.sum(jnp.exp2(terms - top[None]), axis=0)]
    all_to_all x3 -> x2, starting transfers between devices: 21.6 us -> 15.7 us  [the longest x1 9.29 us: per_device(): lax.all_to_all(best.reshape(devices, cap), ('doc', 'cent'), split_axis=0,...]
  transfers between devices with their start and end apart: 4 -> 17, of which waited for: 4 -> 7; matrix products, arithmetic and copies ran while one was open for 8% -> 0% of each run, Pallas kernels for 0% -> 23%
where the time goes in v1:
time: 148 us; the launch traced here: 147 us
  waiting for transfers between devices  64.1 us (43%)
  Pallas kernels  40.2 us (27%)
  starting transfers between devices  33.2 us (22%)
  local copies, waits for them, and re-layouts  7.01 us (5%)
    ppermute x9, waiting for transfers between devices, move_z(): lax.ppermute(value, ('doc', 'cent'), moves(lambda x, y, z, core: (x, y, (...  53 us
    pallas_call x2, Pallas kernels, score(): pl.pallas_call(functools.partial(score_kernel, len(rows), len(centres), 2...  30.3 us
    ppermute x9, starting transfers between devices, move_z(): lax.ppermute(value, ('doc', 'cent'), moves(lambda x, y, z, core: (x, y, (...  13.6 us
    all_to_all x1, starting transfers between devices, per_device(): lax.all_to_all(best.reshape(devices, cap), ('doc', 'cent'), split_axis=0,...  9.29 us
    all_to_all x1, waiting for transfers between devices, per_device(): lax.all_to_all(best.reshape(devices, cap), ('doc', 'cent'), split_axis=0,...  8.78 us
    all_to_all x1, starting transfers between devices, per_device(): lax.all_to_all(send.reshape(devices, cap, width + ID_LANES), ('doc', 'cen...  6.37 us
    unnamed x22, local copies, waits for them, and re-layouts  5.79 us
    pallas_call x1, Pallas kernels, prepare_centres(): pl.pallas_call(centre_kernel, grid=(4,), out_shape=(half, half), in_specs...  4.15 us
  transfers between devices with their start and end apart: 17, of which 7 were waited for; matrix products, arithmetic and copies ran while one was open for 0% of the time, Pallas kernels for 23%

profile of v1, /device:TPU:0, one launch (start us, length us, event | category | flops | bytes accessed | tf_op | source)
XLA Modules:
  0.0 146.6 jit_solution(17488684171429834939)
XLA Ops:
  0.7 4.2 %prepare_centres.1 = (bf16[512,1024]{1,0:T(8,128)(2,1)S(1)}, bf16[512,1024]{1,0:T(8,128)(2,1)}) custom-call(f32[1024,1024]{1,0:T(8,128)} %cen_ref.1), custom_call_target="tpu_custom_call" | custom-call | flops 4194304 | bytes 6291456 | tf_op jit(solution)/shard_map/prepare_centres/pallas_call | solution.py:90
  4.8 1.6 %collective-permute-start.6 = (bf16[512,1024]{1,0:T(8,128)(2,1)S(1)}, bf16[512,1024]{1,0:T(8,128)(2,1)}, u32[]{:S(2)}, u32[]{:S(2)}) collective-permute-start(bf16[512,1024]{1,0:T(8,128)(2,1)S(1)} %get-tuple-element.9.refs_6_.refs_2_), channel_id=1, source_target_pairs={{0,2},{1,3},{4,6},{5,7},{8,10},{9,11},{12,14},{13,15},{2,16},{3,17... | collective-permute-start | bytes 3145736 | tf_op jit(solution)/shard_map/ppermute | solution.py:264
  6.4 1.7 %collective-permute-start.7 = (bf16[512,1024]{1,0:T(8,128)(2,1)}, bf16[512,1024]{1,0:T(8,128)(2,1)}, u32[]{:S(2)}, u32[]{:S(2)}) collective-permute-start(bf16[512,1024]{1,0:T(8,128)(2,1)} %get-tuple-element.10.refs_7_.refs_3_), channel_id=1, source_target_pairs={{0,18},{1,19},{4,22},{5,23},{8,26},{9,27},{12,30},{13,31},{2,0},{3... | collective-permute-start | bytes 3145736 | tf_op jit(solution)/shard_map/ppermute | solution.py:264
  8.1 3.2 %prepare_rows.1 = (bf16[256,1024]{1,0:T(8,128)(2,1)}, bf16[256,1024]{1,0:T(8,128)(2,1)S(1)}, bf16[1024,1152]{1,0:T(8,128)(2,1)}) custom-call(f32[512,1024]{1,0:T(8,128)S(1)} %copy-done.2, s32[1,512]{1,0:T(1,128)S(1)} %bitcast.10, s32[1,512]{1,0:T(1,128)S(1)} %bitcast.12), custom_call_target="tpu_custom_call" | custom-call | flops 1073741824 | bytes 3145728 | tf_op jit(solution)/shard_map/prepare_rows/pallas_call | solution.py:59
  11.2 2.0 %collective-permute-start = (bf16[256,1024]{1,0:T(8,128)(2,1)}, bf16[256,1024]{1,0:T(8,128)(2,1)S(1)}, u32[]{:S(2)}, u32[]{:S(2)}) collective-permute-start(bf16[256,1024]{1,0:T(8,128)(2,1)} %get-tuple-element.7.refs_0_), channel_id=1, source_target_pairs={{0,4},{1,5},{4,8},{5,9},{8,12},{9,13},{12,0},{13,1},{2,6},{3,7},{6... | collective-permute-start | bytes 1572872 | tf_op jit(solution)/shard_map/ppermute | solution.py:270
  13.2 2.1 %collective-permute-start.3 = (bf16[256,1024]{1,0:T(8,128)(2,1)S(1)}, bf16[256,1024]{1,0:T(8,128)(2,1)S(1)}, u32[]{:S(2)}, u32[]{:S(2)}) collective-permute-start(bf16[256,1024]{1,0:T(8,128)(2,1)S(1)} %get-tuple-element.8.refs_1_), channel_id=1, source_target_pairs={{0,12},{1,13},{4,0},{5,1},{8,4},{9,5},{12,8},{13,9},{2,14},{3,15},... | collective-permute-start | bytes 1572872 | tf_op jit(solution)/shard_map/ppermute | solution.py:270
  15.4 0.0 collective-permute-start.1
  15.4 0.8 copy-done.7
  16.2 12.2 %collective-permute-done.refs_2_ = bf16[256,1024]{1,0:T(8,128)(2,1)S(1)} collective-permute-done((bf16[256,1024]{1,0:T(8,128)(2,1)}, bf16[256,1024]{1,0:T(8,128)(2,1)S(1)}, u32[]{:S(2)}, u32[]{:S(2)}) %collective-permute-start) | collective-permute-done | bytes 524320 | tf_op jit(solution)/shard_map/ppermute | solution.py:270
  28.4 0.0 collective-permute-start.4
  28.4 0.0 collective-permute-done.3.refs_5_
  28.4 0.5 collective-permute-start.5
  28.9 2.0 %collective-permute-done.6.refs_10_.refs_6_ = bf16[512,1024]{1,0:T(8,128)(2,1)} collective-permute-done((bf16[512,1024]{1,0:T(8,128)(2,1)S(1)}, bf16[512,1024]{1,0:T(8,128)(2,1)}, u32[]{:S(2)}, u32[]{:S(2)}) %collective-permute-start.6) | collective-permute-done | bytes 1048608 | tf_op jit(solution)/shard_map/ppermute | solution.py:264
  30.9 0.0 collective-permute-start.8
  30.9 0.4 collective-permute-done.7.refs_11_.refs_7_
  31.3 0.1 collective-permute-start.9
  31.4 6.7 %collective-permute-done.1.refs_3_ = bf16[256,1024]{1,0:T(8,128)(2,1)S(1)} collective-permute-done((bf16[256,1024]{1,0:T(8,128)(2,1)S(1)}, bf16[256,1024]{1,0:T(8,128)(2,1)S(1)}, u32[]{:S(2)}, u32[]{:S(2)}) %collective-permute-start.1) | collective-permute-done | bytes 524320 | tf_op jit(solution)/shard_map/ppermute | solution.py:270
  38.2 0.8 copy-done.9
  39.0 1.7 %collective-permute-start.2 = (bf16[256,1024]{1,0:T(8,128)(2,1)}, bf16[256,1024]{1,0:T(8,128)(2,1)}, u32[]{:S(2)}, u32[]{:S(2)}) collective-permute-start(bf16[256,1024]{1,0:T(8,128)(2,1)} %get-tuple-element.7.refs_0_), channel_id=1, source_target_pairs={{0,12},{1,13},{4,0},{5,1},{8,4},{9,5},{12,8},{13,9},{2,14},{3,15},... | collective-permute-start | bytes 1572872 | tf_op jit(solution)/shard_map/ppermute | solution.py:270
  40.7 6.4 %all-to-all-start = ((bf16[128,8,1152]{2,1,0:T(8,128)(2,1)}), bf16[128,8,1152]{2,1,0:T(8,128)(2,1)S(1)}, u32[]{:S(2)}, u32[]{:S(2)}) async-start(bf16[128,8,1152]{2,1,0:T(8,128)(2,1)} %bitcast.3), calls=%async_computation | async-start | bytes 4718592 | tf_op jit(solution)/shard_map/all_to_all | solution.py:288
  47.1 30.4 %collective-permute-done.2.refs_4_ = bf16[256,1024]{1,0:T(8,128)(2,1)} collective-permute-done((bf16[256,1024]{1,0:T(8,128)(2,1)}, bf16[256,1024]{1,0:T(8,128)(2,1)}, u32[]{:S(2)}, u32[]{:S(2)}) %collective-permute-start.2) | collective-permute-done | bytes 524320 | tf_op jit(solution)/shard_map/ppermute | solution.py:270
  77.6 0.0 collective-permute-start.12
  77.6 0.0 collective-permute-done.4.refs_8_.refs_4_
  77.6 3.8 %collective-permute-start.13 = (bf16[256,1024]{1,0:T(8,128)(2,1)}, bf16[256,1024]{1,0:T(8,128)(2,1)S(1)}, u32[]{:S(2)}, u32[]{:S(2)}) collective-permute-start(bf16[256,1024]{1,0:T(8,128)(2,1)} %copy-done.5), channel_id=1, source_target_pairs={{0,12},{1,13},{4,0},{5,1},{8,4},{9,5},{12,8},{13,9},{2,14},{3,15},... | collective-permute-start | bytes 1572872 | tf_op jit(solution)/shard_map/ppermute | solution.py:270
  81.4 0.0 collective-permute-done.5.refs_9_.refs_5_
  81.4 0.0 collective-permute-done.8.refs_12_.refs_8_
  81.4 0.0 collective-permute-done.9.refs_13_.refs_9_
  81.4 1.0 copy-done.4
  82.5 1.0 copy-done.6
  83.5 1.0 copy-done.8
  84.5 1.0 copy-done.10
  85.6 20.9 %score_near.1 = f32[1,1536]{1,0:T(1,128)S(1)} custom-call(bf16[256,1024]{1,0:T(8,128)(2,1)} %get-tuple-element.7.refs_0_, bf16[256,1024]{1,0:T(8,128)(2,1)S(1)} %copy-done.8, bf16[256,1024]{1,0:T(8,128)(2,1)S(1)} %copy-done.4, bf16[256,1024]{1,0:T(8,128)(2,1)S(1)} %copy-done.10, bf16[256,1024]{1,0:T(8,128)(2,1)} %collective-permute-done.2.refs_4_, ...), custom_call_target="tpu_custom_call" | custom-call | flops 12884901888 | bytes 11534336 | tf_op jit(solution)/shard_map/score_near/pallas_call | solution.py:152
  106.5 2.1 %collective-permute-start.10 = (f32[1,512]{1,0:T(1,128)S(1)}, f32[1,512]{1,0:T(1,128)S(1)}, u32[]{:S(2)}, u32[]{:S(2)}) collective-permute-start(f32[1,512]{1,0:T(1,128)S(1)} %get-tuple-element.14), channel_id=1, source_target_pairs={{0,12},{1,13},{4,0},{5,1},{8,4},{9,5},{12,8},{13,9},{2,14},{3,15},... | collective-permute-start | bytes 6152 | tf_op jit(solution)/shard_map/ppermute | solution.py:270
  108.5 0.0 collective-permute-start.11
  108.5 0.0 collective-permute-done.12.refs_0_
  108.6 0.0 collective-permute-done.13.refs_1_
  108.6 9.5 %score_far.1 = f32[1,512]{1,0:T(1,128)S(1)} custom-call(bf16[256,1024]{1,0:T(8,128)(2,1)S(1)} %collective-permute-done.12.refs_0_, bf16[256,1024]{1,0:T(8,128)(2,1)S(1)} %collective-permute-done.13.refs_1_, bf16[512,1024]{1,0:T(8,128)(2,1)S(1)} %get-tuple-element.9.refs_6_.refs_2_, bf16[512,1024]{1,0:T(8,128)(2,1)} %get-tuple-element.10.refs_7_.refs_3_, ...), custom_call_target="tpu_custom_call" | custom-call | flops 4294967296 | bytes 9437184 | tf_op jit(solution)/shard_map/score_far/pallas_call | solution.py:152
  118.0 1.8 %collective-permute-start.14 = (f32[1,512]{1,0:T(1,128)S(1)}, f32[1,512]{1,0:T(1,128)S(1)}, u32[]{:S(2)}, u32[]{:S(2)}) collective-permute-start(f32[1,512]{1,0:T(1,128)S(1)} %score_far.1), channel_id=1, source_target_pairs={{0,8},{1,9},{4,12},{5,13},{8,0},{9,1},{12,4},{13,5},{2,10},{3,11},... | collective-permute-start | bytes 6152 | tf_op jit(solution)/shard_map/ppermute | solution.py:270
  119.9 0.0 collective-permute-done.10
  119.9 3.5 %collective-permute-done.14 = f32[1,512]{1,0:T(1,128)S(1)} collective-permute-done((f32[1,512]{1,0:T(1,128)S(1)}, f32[1,512]{1,0:T(1,128)S(1)}, u32[]{:S(2)}, u32[]{:S(2)}) %collective-permute-start.14) | collective-permute-done | bytes 2080 | tf_op jit(solution)/shard_map/ppermute | solution.py:270
  123.5 1.7 %owner_best.1 = f32[1,1024]{1,0:T(1,128)S(1)} custom-call(bf16[1024,1152]{1,0:T(8,128)(2,1)S(1)} %bitcast.8), custom_call_target="tpu_custom_call" | custom-call | flops 2415919104 | bytes 2359296 | tf_op jit(solution)/shard_map/owner_best/pallas_call | solution.py:204
  125.2 0.5 broadcast.3
  125.7 0.7 reduce.7
  126.3 0.7 all_to_all.11
  127.0 9.3 %all-to-all-start.1 = ((f32[128,1,8]{2,1,0:T(1,128)}), f32[128,1,8]{2,1,0:T(1,128)S(1)}, u32[]{:S(2)}, u32[]{:S(2)}) async-start(f32[128,1,8]{2,1,0:T(1,128)} %bitcast.5), calls=%async_computation.1 | async-start | bytes 131072 | tf_op jit(solution)/shard_map/all_to_all | solution.py:316
  136.3 0.6 multiply_subtract_fusion
  136.9 8.8 %all-to-all-done.1 = f32[128,1,8]{2,1,0:T(1,128)S(1)} async-done(((f32[128,1,8]{2,1,0:T(1,128)}), f32[128,1,8]{2,1,0:T(1,128)S(1)}, u32[]{:S(2)}, u32[]{:S(2)}) %all-to-all-start.1) | async-done | bytes 4128 | tf_op jit(solution)/shard_map/all_to_all | solution.py:316
  145.7 0.9 pick.1
  (21 shorter events, 0.1 us)
Async XLA Ops:
  0.6 7.4 %copy-start = (s32[512]{0:T(512)S(1)}, s32[512]{0:T(512)}, u32[]{:S(2)}) copy-start(s32[512]{0:T(512)} %param.6) | copy-start | bytes 6148
  0.6 7.4 %copy-start.1 = (s32[512]{0:T(512)S(1)}, s32[512]{0:T(512)}, u32[]{:S(2)}) copy-start(s32[512]{0:T(512)} %param.7) | copy-start | bytes 6148
  0.7 7.4 %copy-start.2 = (f32[512,1024]{1,0:T(8,128)S(1)}, f32[512,1024]{1,0:T(8,128)}, u32[]{:S(2)}) copy-start(f32[512,1024]{1,0:T(8,128)} %emb_ref.1) | copy-start | bytes 6291460
  4.8 26.1 %collective-permute-start.6 = (bf16[512,1024]{1,0:T(8,128)(2,1)S(1)}, bf16[512,1024]{1,0:T(8,128)(2,1)}, u32[]{:S(2)}, u32[]{:S(2)}) collective-permute-start(bf16[512,1024]{1,0:T(8,128)(2,1)S(1)} %get-tuple-element.9.refs_6_.refs_2_), channel_id=1, source_target_pairs={{0,2},{1,3},{4,6},{5,7},{8,10},{9,11},{12,14},{13,15},{2,16},{3,17... | collective-permute-start | bytes 3145736 | tf_op jit(solution)/shard_map/ppermute | solution.py:264
  6.4 24.9 %collective-permute-start.7 = (bf16[512,1024]{1,0:T(8,128)(2,1)}, bf16[512,1024]{1,0:T(8,128)(2,1)}, u32[]{:S(2)}, u32[]{:S(2)}) collective-permute-start(bf16[512,1024]{1,0:T(8,128)(2,1)} %get-tuple-element.10.refs_7_.refs_3_), channel_id=1, source_target_pairs={{0,18},{1,19},{4,22},{5,23},{8,26},{9,27},{12,30},{13,31},{2,0},{3... | collective-permute-start | bytes 3145736 | tf_op jit(solution)/shard_map/ppermute | solution.py:264
  11.2 17.2 %collective-permute-start = (bf16[256,1024]{1,0:T(8,128)(2,1)}, bf16[256,1024]{1,0:T(8,128)(2,1)S(1)}, u32[]{:S(2)}, u32[]{:S(2)}) collective-permute-start(bf16[256,1024]{1,0:T(8,128)(2,1)} %get-tuple-element.7.refs_0_), channel_id=1, source_target_pairs={{0,4},{1,5},{4,8},{5,9},{8,12},{9,13},{12,0},{13,1},{2,6},{3,7},{6... | collective-permute-start | bytes 1572872 | tf_op jit(solution)/shard_map/ppermute | solution.py:270
  13.2 15.2 %collective-permute-start.3 = (bf16[256,1024]{1,0:T(8,128)(2,1)S(1)}, bf16[256,1024]{1,0:T(8,128)(2,1)S(1)}, u32[]{:S(2)}, u32[]{:S(2)}) collective-permute-start(bf16[256,1024]{1,0:T(8,128)(2,1)S(1)} %get-tuple-element.8.refs_1_), channel_id=1, source_target_pairs={{0,12},{1,13},{4,0},{5,1},{8,4},{9,5},{12,8},{13,9},{2,14},{3,15},... | collective-permute-start | bytes 1572872 | tf_op jit(solution)/shard_map/ppermute | solution.py:270
  15.4 22.8 %collective-permute-start.1 = (bf16[256,1024]{1,0:T(8,128)(2,1)S(1)}, bf16[256,1024]{1,0:T(8,128)(2,1)S(1)}, u32[]{:S(2)}, u32[]{:S(2)}) collective-permute-start(bf16[256,1024]{1,0:T(8,128)(2,1)S(1)} %get-tuple-element.8.refs_1_), channel_id=1, source_target_pairs={{0,4},{1,5},{4,8},{5,9},{8,12},{9,13},{12,0},{13,1},{2,6},{3,7},{6... | collective-permute-start | bytes 1572872 | tf_op jit(solution)/shard_map/ppermute | solution.py:270
  15.4 0.8 copy-start.7
  28.4 2.5 %copy-start.3 = (bf16[256,1024]{1,0:T(8,128)(2,1)}, bf16[256,1024]{1,0:T(8,128)(2,1)S(1)}, u32[]{:S(2)}) copy-start(bf16[256,1024]{1,0:T(8,128)(2,1)S(1)} %collective-permute-done.refs_2_) | copy-start | bytes 1572868
  28.4 49.2 %collective-permute-start.4 = (bf16[512,1024]{1,0:T(8,128)(2,1)S(1)}, bf16[512,1024]{1,0:T(8,128)(2,1)}, u32[]{:S(2)}, u32[]{:S(2)}) collective-permute-start(bf16[512,1024]{1,0:T(8,128)(2,1)S(1)} %get-tuple-element.9.refs_6_.refs_2_), channel_id=1, source_target_pairs={{0,1},{1,0},{4,5},{5,4},{8,9},{9,8},{12,13},{13,12},{2,3},{3,2},{6... | collective-permute-start | bytes 3145736 | tf_op jit(solution)/shard_map/ppermute | solution.py:274
  28.4 2.5 %copy-start.5 = (bf16[256,1024]{1,0:T(8,128)(2,1)}, bf16[256,1024]{1,0:T(8,128)(2,1)S(1)}, u32[]{:S(2)}) copy-start(bf16[256,1024]{1,0:T(8,128)(2,1)S(1)} %collective-permute-done.3.refs_5_) | copy-start | bytes 1572868
  28.4 53.0 %collective-permute-start.5 = (bf16[512,1024]{1,0:T(8,128)(2,1)}, bf16[512,1024]{1,0:T(8,128)(2,1)}, u32[]{:S(2)}, u32[]{:S(2)}) collective-permute-start(bf16[512,1024]{1,0:T(8,128)(2,1)} %get-tuple-element.10.refs_7_.refs_3_), channel_id=1, source_target_pairs={{0,1},{1,0},{4,5},{5,4},{8,9},{9,8},{12,13},{13,12},{2,3},{3,2},{6... | collective-permute-start | bytes 3145736 | tf_op jit(solution)/shard_map/ppermute | solution.py:274
  30.9 50.5 %collective-permute-start.8 = (bf16[512,1024]{1,0:T(8,128)(2,1)}, bf16[512,1024]{1,0:T(8,128)(2,1)}, u32[]{:S(2)}, u32[]{:S(2)}) collective-permute-start(bf16[512,1024]{1,0:T(8,128)(2,1)} %collective-permute-done.6.refs_10_.refs_6_), channel_id=1, source_target_pairs={{0,1},{1,0},{4,5},{5,4},{8,9},{9,8},{12,13},{13,12},{2,3},{3,2},{6... | collective-permute-start | bytes 3145736 | tf_op jit(solution)/shard_map/ppermute | solution.py:274
  31.3 50.1 %collective-permute-start.9 = (bf16[512,1024]{1,0:T(8,128)(2,1)}, bf16[512,1024]{1,0:T(8,128)(2,1)}, u32[]{:S(2)}, u32[]{:S(2)}) collective-permute-start(bf16[512,1024]{1,0:T(8,128)(2,1)} %collective-permute-done.7.refs_11_.refs_7_), channel_id=1, source_target_pairs={{0,1},{1,0},{4,5},{5,4},{8,9},{9,8},{12,13},{13,12},{2,3},{3,2},{6... | collective-permute-start | bytes 3145736 | tf_op jit(solution)/shard_map/ppermute | solution.py:274
  38.2 0.8 copy-start.9
  39.0 38.6 %collective-permute-start.2 = (bf16[256,1024]{1,0:T(8,128)(2,1)}, bf16[256,1024]{1,0:T(8,128)(2,1)}, u32[]{:S(2)}, u32[]{:S(2)}) collective-permute-start(bf16[256,1024]{1,0:T(8,128)(2,1)} %get-tuple-element.7.refs_0_), channel_id=1, source_target_pairs={{0,12},{1,13},{4,0},{5,1},{8,4},{9,5},{12,8},{13,9},{2,14},{3,15},... | collective-permute-start | bytes 1572872 | tf_op jit(solution)/shard_map/ppermute | solution.py:270
  40.7 82.7 %all-to-all-start = ((bf16[128,8,1152]{2,1,0:T(8,128)(2,1)}), bf16[128,8,1152]{2,1,0:T(8,128)(2,1)S(1)}, u32[]{:S(2)}, u32[]{:S(2)}) async-start(bf16[128,8,1152]{2,1,0:T(8,128)(2,1)} %bitcast.3), calls=%async_computation | async-start | bytes 4718592 | tf_op jit(solution)/shard_map/all_to_all | solution.py:288
  77.6 31.0 %collective-permute-start.12 = (bf16[256,1024]{1,0:T(8,128)(2,1)}, bf16[256,1024]{1,0:T(8,128)(2,1)S(1)}, u32[]{:S(2)}, u32[]{:S(2)}) collective-permute-start(bf16[256,1024]{1,0:T(8,128)(2,1)} %copy-done.3), channel_id=1, source_target_pairs={{0,4},{1,5},{4,8},{5,9},{8,12},{9,13},{12,0},{13,1},{2,6},{3,7},{6... | collective-permute-start | bytes 1572872 | tf_op jit(solution)/shard_map/ppermute | solution.py:270
  77.6 31.0 %collective-permute-start.13 = (bf16[256,1024]{1,0:T(8,128)(2,1)}, bf16[256,1024]{1,0:T(8,128)(2,1)S(1)}, u32[]{:S(2)}, u32[]{:S(2)}) collective-permute-start(bf16[256,1024]{1,0:T(8,128)(2,1)} %copy-done.5), channel_id=1, source_target_pairs={{0,12},{1,13},{4,0},{5,1},{8,4},{9,5},{12,8},{13,9},{2,14},{3,15},... | collective-permute-start | bytes 1572872 | tf_op jit(solution)/shard_map/ppermute | solution.py:270
  81.4 1.0 copy-start.4
  82.5 1.0 copy-start.6
  83.5 1.0 copy-start.8
  84.5 1.0 copy-start.10
  106.5 13.4 %collective-permute-start.10 = (f32[1,512]{1,0:T(1,128)S(1)}, f32[1,512]{1,0:T(1,128)S(1)}, u32[]{:S(2)}, u32[]{:S(2)}) collective-permute-start(f32[1,512]{1,0:T(1,128)S(1)} %get-tuple-element.14), channel_id=1, source_target_pairs={{0,12},{1,13},{4,0},{5,1},{8,4},{9,5},{12,8},{13,9},{2,14},{3,15},... | collective-permute-start | bytes 6152 | tf_op jit(solution)/shard_map/ppermute | solution.py:270
  108.5 11.3 %collective-permute-start.11 = (f32[1,512]{1,0:T(1,128)S(1)}, f32[1,512]{1,0:T(1,128)S(1)}, u32[]{:S(2)}, u32[]{:S(2)}) collective-permute-start(f32[1,512]{1,0:T(1,128)S(1)} %get-tuple-element.15), channel_id=1, source_target_pairs={{0,4},{1,5},{4,8},{5,9},{8,12},{9,13},{12,0},{13,1},{2,6},{3,7},{6... | collective-permute-start | bytes 6152 | tf_op jit(solution)/shard_map/ppermute | solution.py:270
  118.0 5.4 %collective-permute-start.14 = (f32[1,512]{1,0:T(1,128)S(1)}, f32[1,512]{1,0:T(1,128)S(1)}, u32[]{:S(2)}, u32[]{:S(2)}) collective-permute-start(f32[1,512]{1,0:T(1,128)S(1)} %score_far.1), channel_id=1, source_target_pairs={{0,8},{1,9},{4,12},{5,13},{8,0},{9,1},{12,4},{13,5},{2,10},{3,11},... | collective-permute-start | bytes 6152 | tf_op jit(solution)/shard_map/ppermute | solution.py:270
  127.0 18.7 %all-to-all-start.1 = ((f32[128,1,8]{2,1,0:T(1,128)}), f32[128,1,8]{2,1,0:T(1,128)S(1)}, u32[]{:S(2)}, u32[]{:S(2)}) async-start(f32[128,1,8]{2,1,0:T(1,128)} %bitcast.5), calls=%async_computation.1 | async-start | bytes 131072 | tf_op jit(solution)/shard_map/all_to_all | solution.py:316

commit v2 on v0

v2 whole, which is shorter than its diff:
```python
import functools
import math

import jax
import jax.numpy as jnp
from jax import lax
from jax.experimental import pallas as pl
from jax.experimental.pallas import tpu as pltpu
from jax.sharding import PartitionSpec as P

INVERSE_TEMP = 256.0
SCALE = INVERSE_TEMP / math.log(2.0)
BACK = math.log(2.0) / INVERSE_TEMP
NT = (((1,), (1,)), ((), ()))
ID_LANES = 128
LANES = 256
VMEM = pl.BlockSpec(memory_space=pltpu.VMEM)
TINY = pl.CostEstimate(flops=1, bytes_accessed=1, transcendentals=0)


PARAMS = pltpu.CompilerParams(vmem_limit_bytes=60 * 1024 * 1024)
SCORE_PARAMS = pltpu.CompilerParams(vmem_limit_bytes=24 * 1024 * 1024)
ANY = pl.BlockSpec(memory_space=pl.ANY)
CHUNK = 128
STEP = 512


def unit_of(values):
    total = jnp.sum(values * values, axis=1, keepdims=True)
    return (values * lax.rsqrt(total + 1e-06)).astype(jnp.bfloat16)


def prepare_kernel(per_owner, cap, *refs):
    emb_hbm, cen_hbm, cluster_hbm, slot_hbm = refs[:4]
    unit_hbm, send_hbm, centre_hbm = refs[4:7]
    emb, cen, cluster_ref, slot_ref, unit_ref, send_ref, centre_ref = refs[7:14]
    emb_sems, cen_sems, id_sems, unit_sems, send_sems, centre_sems = refs[14:]
    rows, width = emb.shape

    def copy_of(src, dst, sem):
        return pltpu.make_async_copy(src, dst, sem)

    def piece(ref, i, size=CHUNK):
        return ref.at[pl.ds(i * size, size)]

    ids = [
        copy_of(cluster_hbm, cluster_ref, id_sems.at[0]),
        copy_of(slot_hbm, slot_ref, id_sems.at[1]),
    ]
    emb_copies = [
        copy_of(piece(emb_hbm, i), piece(emb, i), emb_sems.at[i]) for i in range(rows // CHUNK)
    ]
    cen_copies = [
        copy_of(piece(cen_hbm, i), piece(cen, i), cen_sems.at[i])
        for i in range(cen.shape[0] // CHUNK)
    ]
    for copy in emb_copies + ids + cen_copies:
        copy.start()
    out = []

    def send_out(src, dst, sem):
        out.append(copy_of(src, dst, sem))
        out[-1].start()

    for i, copy in enumerate(emb_copies):
        copy.wait()
        part = slice(i * CHUNK, (i + 1) * CHUNK)
        unit_ref[part] = unit_of(emb[part])
        send_out(piece(unit_ref, i), piece(unit_hbm, i), unit_sems.at[i])
    for copy in ids:
        copy.wait()
    cluster = cluster_ref[...]
    target = (cluster // per_owner) * cap + slot_ref[...]
    local = (cluster % per_owner + 1).astype(jnp.float32)
    names = jnp.broadcast_to(local, (ID_LANES, rows)).astype(jnp.bfloat16)
    for i in range(send_ref.shape[0] // LANES):
        part = slice(i * LANES, (i + 1) * LANES)
        place = i * LANES + lax.broadcasted_iota(jnp.int32, (LANES, rows), 0)
        hot = (place == target).astype(jnp.float32).astype(jnp.bfloat16)
        send_ref[part, :width] = lax.dot_general(
            hot, unit_ref[...], (((1,), (0,)), ((), ())), preferred_element_type=jnp.float32
        ).astype(jnp.bfloat16)
        send_ref[part, width:] = (
            lax.dot_general(hot, names, NT, preferred_element_type=jnp.float32) - 1.0
        ).astype(jnp.bfloat16)
        send_out(piece(send_ref, i, LANES), piece(send_hbm, i, LANES), send_sems.at[i])
    for i, copy in enumerate(cen_copies):
        copy.wait()
        part = slice(i * CHUNK, (i + 1) * CHUNK)
        centre_ref[part] = unit_of(cen[part])
        send_out(piece(centre_ref, i), piece(centre_hbm, i), centre_sems.at[i])
    for copy in out:
        copy.wait()


def prepare(embeddings, centroids, cluster, slot, per_owner, cap, devices):
    rows, width = embeddings.shape
    count = centroids.shape[0]
    send = (devices * cap, width + ID_LANES)
    shapes = ((rows, width), send, (count, width))
    sems = (rows // CHUNK, count // CHUNK, 2, rows // CHUNK, send[0] // LANES)
    sems += (count // CHUNK,)
    return pl.pallas_call(
        functools.partial(prepare_kernel, per_owner, cap),
        out_shape=tuple(jax.ShapeDtypeStruct(shape, jnp.bfloat16) for shape in shapes),
        in_specs=[ANY] * 4,
        out_specs=(ANY,) * 3,
        scratch_shapes=[
            pltpu.VMEM((rows, width), jnp.float32),
            pltpu.VMEM((count, width), jnp.float32),
            pltpu.VMEM((1, rows), jnp.int32),
            pltpu.VMEM((1, rows), jnp.int32),
            pltpu.VMEM((rows, width), jnp.bfloat16),
            pltpu.VMEM(send, jnp.bfloat16),
            pltpu.VMEM((count, width), jnp.bfloat16),
        ]
        + [pltpu.SemaphoreType.DMA((n,)) for n in sems],
        compiler_params=PARAMS,
        cost_estimate=TINY,
        name="prepare",
    )(embeddings, centroids, cluster.reshape(1, rows), slot.reshape(1, rows))


def score_kernel(n_rows, sizes, fetch, plan, *refs):
    n_cent = len(sizes)
    row_refs, refs = refs[:n_rows], refs[n_rows:]
    if fetch:
        cent_refs, (out_ref, table), refs = refs[:n_cent], refs[n_cent : n_cent + 2], refs[n_cent + 2 :]
    else:
        cent_refs, (table, out_ref), refs = (), refs[:2], refs[2:]
    rows, high, total, row_sems, cent_sems = refs

    def copies_of(arrays, buffer, sems):
        copies, i, base = [], 0, 0
        for ref in arrays:
            mine = []
            size = min(STEP, ref.shape[0])
            for start in range(0, ref.shape[0], size):
                mine.append(
                    pltpu.make_async_copy(
                        ref.at[pl.ds(start, size)], buffer.at[pl.ds(base + start, size)], sems.at[i]
                    )
                )
                i += 1
            copies.append(mine)
            base += ref.shape[0]
        return copies

    row_starts = [sum(ref.shape[0] for ref in row_refs[:j]) for j in range(n_rows)]
    cent_starts = [sum(sizes[:i]) for i in range(n_cent)]
    row_copies = copies_of(row_refs, rows, row_sems)
    cent_copies = copies_of(cent_refs, table, cent_sems)
    stages = [
        [copy for j in new_rows for copy in row_copies[j]]
        + [copy for i in new_cents if fetch for copy in cent_copies[i]]
        for new_rows, new_cents, _ in plan
    ]

    def product(cent, lanes):
        return lax.dot_general(
            table[pl.ds(cent, STEP)], rows[lanes], NT, preferred_element_type=jnp.float32
        )

    for copy in stages[0]:
        copy.start()
    begun = set()
    for k, (_, _, products) in enumerate(plan):
        for copy in stages[k]:
            copy.wait()
        for copy in stages[k + 1] if k + 1 < len(plan) else []:
            copy.start()
        for i, j in products:
            for row in range(row_starts[j], row_starts[j] + row_refs[j].shape[0], LANES):
                lanes = slice(row, row + LANES)
                for cent in range(cent_starts[i], cent_starts[i] + sizes[i], STEP):
                    value = product(cent, lanes) * SCALE
                    if row not in begun:
                        shift = jnp.max(value, axis=0, keepdims=True)
                        high[:, lanes] = jnp.broadcast_to(shift, (8, LANES))
                    value = jnp.exp2(value.reshape(STEP // 8, 8, LANES) - high[:, lanes][None])
                    value = jnp.sum(value, axis=0)
                    total[:, lanes] = value if row not in begun else total[:, lanes] + value
                    begun.add(row)

    @pl.when(jnp.logical_not(jnp.max(total[...]) < 1e38))
    def _():
        high[...] = jnp.full_like(high, -1e30)
        total[...] = jnp.zeros_like(total)
        for i, j in [pair for _, _, products in plan for pair in products]:

            @pl.loop(0, row_refs[j].shape[0] // LANES)
            def _(r):
                @pl.loop(0, sizes[i] // STEP)
                def _(c):
                    lanes = pl.ds(pl.multiple_of(row_starts[j] + r * LANES, LANES), LANES)
                    value = product(pl.multiple_of(cent_starts[i] + c * STEP, STEP), lanes) * SCALE
                    value = value.reshape(STEP // 8, 8, LANES)
                    before = high[:, lanes]
                    now = jnp.maximum(before, jnp.max(value, axis=0))
                    high[:, lanes] = now
                    total[:, lanes] = total[:, lanes] * jnp.exp2(before - now) + jnp.sum(
                        jnp.exp2(value - now[None]), axis=0
                    )

    top = jnp.max(high[...], axis=0, keepdims=True)
    all_sum = jnp.sum(total[...] * jnp.exp2(high[...] - top), axis=0, keepdims=True)
    out_ref[...] = top + jnp.log2(all_sum)


def score(rows, centres, plan, name, sizes=None):
    fetch = sizes is None
    if fetch:
        sizes = tuple(value.shape[0] for value in centres)
    width = rows[0].shape[1]
    count = sum(value.shape[0] for value in rows)
    out = jax.ShapeDtypeStruct((1, count), jnp.float32)
    table = jax.ShapeDtypeStruct((sum(sizes), width), jnp.bfloat16)
    return pl.pallas_call(
        functools.partial(score_kernel, len(rows), sizes, fetch, plan),
        out_shape=(out, table) if fetch else out,
        in_specs=[ANY] * len(rows) + ([ANY] * len(centres) if fetch else [VMEM]),
        out_specs=(VMEM, VMEM) if fetch else VMEM,
        scratch_shapes=[
            pltpu.VMEM((count, width), jnp.bfloat16),
            pltpu.VMEM((8, count), jnp.float32),
            pltpu.VMEM((8, count), jnp.float32),
            pltpu.SemaphoreType.DMA((count // LANES,)),
            pltpu.SemaphoreType.DMA((sum(sizes) // STEP,)),
        ],
        compiler_params=SCORE_PARAMS,
        cost_estimate=TINY,
        name=name,
    )(*rows, *(centres if fetch else (centres,)))


def owner_kernel(rows_hbm, out_ref, rows_ref, sems):
    total = rows_ref.shape[0]
    width = rows_ref.shape[1] - ID_LANES
    cap = out_ref.shape[1]
    block = LANES
    copies = [
        pltpu.make_async_copy(
            rows_hbm.at[pl.ds(i * block, block)], rows_ref.at[pl.ds(i * block, block)], sems.at[i]
        )
        for i in range(total // block)
    ]
    for copy in copies:
        copy.start()
    pick = (lax.broadcasted_iota(jnp.int32, (8, ID_LANES), 1) == 0).astype(jnp.float32)
    pick = pick.astype(jnp.bfloat16)
    r = lax.broadcasted_iota(jnp.int32, (block, block), 0)
    s = lax.broadcasted_iota(jnp.int32, (block, block), 1)
    eye = lax.broadcasted_iota(jnp.int32, (cap, ID_LANES), 0)
    eye = (eye == lax.broadcasted_iota(jnp.int32, (cap, ID_LANES), 1)).astype(jnp.float32)
    id_rows = []
    for row in range(0, total, block):
        if row in (0, total // 2):
            for copy in copies[row // block : (row + total // 2) // block]:
                copy.wait()
        ids = rows_ref[row : row + block, width:]
        id_rows.append(lax.dot_general(pick, ids, NT, preferred_element_type=jnp.float32)[:1])
        id_col = ids.astype(jnp.float32)
        best = jnp.full((block, ID_LANES), -1.0, jnp.float32)
        for col in range(0, row + block, block):
            gram = lax.dot_general(
                rows_ref[row : row + block, :width],
                rows_ref[col : col + block, :width],
                NT,
                preferred_element_type=jnp.float32,
            )
            for lane in range(0, block, ID_LANES):
                lanes = slice(lane, lane + ID_LANES)
                same = id_col == id_rows[col // block][:, lanes]
                if row == col:
                    same = same & (s < r)[:, lanes]
                best = jnp.maximum(best, jnp.where(same, gram[:, lanes], -1.0))
        best = jnp.max(best, axis=1, keepdims=True).reshape(block // cap, cap, 1)
        best = jnp.sum(best * eye[None], axis=1)
        out_ref[row // cap : (row + block) // cap, :] = best[:, :cap]


def owner_best(rows, cap):
    total, width = rows.shape
    return pl.pallas_call(
        owner_kernel,
        out_shape=jax.ShapeDtypeStruct((total // cap, cap), jnp.float32),
        in_specs=[ANY],
        out_specs=VMEM,
        scratch_shapes=[
            pltpu.VMEM((total, width), jnp.bfloat16),
            pltpu.SemaphoreType.DMA((total // LANES,)),
        ],
        compiler_params=SCORE_PARAMS,
        cost_estimate=TINY,
        name="owner_best",
    )(rows)


def pick_kernel(per_owner, got_ref, cluster_ref, slot_ref, out_ref):
    got = got_ref[...]
    devices, cap = got.shape
    rows = out_ref.shape[1]
    owner = cluster_ref[...] // per_owner
    hot = (lax.broadcasted_iota(jnp.int32, (devices, rows), 0) == owner).astype(jnp.float32)
    by_slot = lax.dot_general(
        got,
        hot,
        (((0,), (0,)), ((), ())),
        precision=lax.Precision.HIGHEST,
        preferred_element_type=jnp.float32,
    )
    mine = lax.broadcasted_iota(jnp.int32, (cap, rows), 0) == slot_ref[...]
    out_ref[...] = jnp.sum(jnp.where(mine, by_slot, 0.0), axis=0, keepdims=True)


def pick(got, cluster, slot, per_owner):
    rows = cluster.shape[0]
    return pl.pallas_call(
        functools.partial(pick_kernel, per_owner),
        out_shape=jax.ShapeDtypeStruct((1, rows), jnp.float32),
        in_specs=[VMEM] * 3,
        out_specs=VMEM,
        compiler_params=SCORE_PARAMS,
        cost_estimate=TINY,
        name="pick",
    )(got, cluster.reshape(1, rows), slot.reshape(1, rows)).reshape(rows)


def move(value, step):
    pairs = []
    for y in range(4):
        for x in range(4):
            for z in range(4):
                for core in range(2):
                    here, there = [
                        (y * 2 + a % 4 // 2) * 16 + (b % 4 * 2 + a % 2) * 2 + c
                        for a, b, c in ((x, z, core), step(x, z, core))
                    ]
                    pairs.append((here, there))
    return lax.ppermute(value, ("doc", "cent"), pairs)


def swap_core(value):
    return move(value, lambda x, z, core: (x, z, 1 - core))


def move_x(value):
    return move(value, lambda x, z, core: (x + 1 - 2 * core, z, core))


def move_z(value, by):
    return move(value, lambda x, z, core: (x, z + by * (1 - 2 * core), core))


def per_device(embeddings, centroids, cluster, slot):
    row_count, width = embeddings.shape
    devices = lax.axis_size("doc") * lax.axis_size("cent")
    per_owner = centroids.shape[0] // lax.axis_size("doc")
    cap = 2 * row_count // devices

    unit, send, centre = prepare(embeddings, centroids, cluster, slot, per_owner, cap, devices)
    ahead, behind = move_z(unit, 1), move_z(unit, -1)
    side, core = move_x(centre), swap_core(centre)
    plan = (((0,), (0,), ((0, 0),)), ((), (1,), ((1, 0),)))
    first, _ = score((unit,), (centre, core), plan, "score_own")

    def after(value, done):
        return lax.optimization_barrier((value, done))[0]

    got = lax.all_to_all(
        send.reshape(devices, cap, width + ID_LANES),
        ("doc", "cent"),
        split_axis=0,
        concat_axis=0,
        tiled=True,
    )
    side, ahead, behind = after(side, first), after(ahead, first), after(behind, first)
    side_core = swap_core(after(side, (ahead, behind)))
    far = move_z(ahead, 1)
    best = owner_best(after(got, first).reshape(devices * cap, width + ID_LANES), cap)
    returned = lax.all_to_all(best, ("doc", "cent"), split_axis=0, concat_axis=0, tiled=True)

    centres = (side, side_core, centre, core)
    plan = (
        ((0, 1), (0,), ((0, 0), (0, 1))),
        ((2,), (1,), ((1, 0), (1, 1), (0, 2), (1, 2))),
        ((), (2, 3), ((2, 1), (2, 2), (3, 1), (3, 2))),
    )
    near, table = score((unit, ahead, after(behind, best)), centres, plan, "score_near")
    parts = [near[:, i * row_count : (i + 1) * row_count] for i in range(3)]
    plan = (((0,), (0, 1, 2, 3), ((0, 0), (1, 0), (2, 0), (3, 0))),)
    sizes = tuple(value.shape[0] for value in centres)
    last = score((far,), table, plan, "score_far", sizes)

    terms = (first, parts[0], move_z(parts[1], -1), move_z(parts[2], 1))
    terms = jnp.concatenate([*terms, move_z(last, 2)], axis=0)
    top = jnp.max(terms, axis=0)
    soft_cost = 1.0 - BACK * (top + jnp.log2(jnp.sum(jnp.exp2(terms - top[None]), axis=0)))
    dup_sim = pick(returned, cluster, slot, per_owner)
    return (soft_cost, dup_sim)


def solution(mesh):
    return jax.shard_map(
        per_device,
        mesh=mesh,
        in_specs=(
            P(("doc", "cent"), None),
            P("cent", None),
            P(("doc", "cent")),
            P(("doc", "cent")),
        ),
        out_specs=(P(("doc", "cent")), P(("doc", "cent"))),
        check_vma=False,
    )
```

time: 261 us -> 141 us (0.54)
  waiting for transfers between devices: 150 us -> 33.2 us
  Pallas kernels: 0 us -> 75.2 us
  matrix products: 35.8 us -> 0 us
  other arithmetic: 24.4 us -> 0.63 us
  between operations: 14.1 us -> 0.78 us
  local copies, waits for them, and re-layouts: 12.2 us -> 3.22 us
  starting transfers between devices: 21.7 us -> 27.8 us
    all_gather x1 -> x0, waiting for transfers between devices: 83 us -> none  [per_device(): lax.all_gather(centre, 'cent', axis=0, tiled=True)]
    pallas_call x0 -> x6, Pallas kernels: none -> 75.2 us  [the longest x3 64.6 us: score(): pl.pallas_call(functools.partial(score_kernel, len(rows), sizes, fetch, p...]
    all_to_all x3 -> x2, waiting for transfers between devices: 67 us -> 5.92 us  [the longest x1 5.91 us: per_device(): lax.all_to_all(send.reshape(devices, cap, width + ID_LANES), ('doc', 'cen...]
    dot_general x3 -> x0, matrix products: 35.8 us -> none  [inner_rows(): lax.dot_general(left, right, (((1,), (1,)), ((), ())), preferred_element_...]
    ppermute x0 -> x9, waiting for transfers between devices: none -> 27.3 us  [move(): return lax.ppermute(value, ('doc', 'cent'), pairs)]
    reduce_sum x3 -> x1, other arithmetic: 17 us -> 0.03 us  [per_device(): jnp.sum(jnp.exp2(terms - top[None]), axis=0)]
    ppermute x0 -> x9, starting transfers between devices: none -> 13.9 us  [move(): return lax.ppermute(value, ('doc', 'cent'), pairs)]
    all_to_all x3 -> x2, starting transfers between devices: 21.6 us -> 13.9 us  [the longest x1 8.75 us: per_device(): lax.all_to_all(send.reshape(devices, cap, width + ID_LANES), ('doc', 'cen...]
  transfers between devices with their start and end apart: 4 -> 11, of which waited for: 4 -> 6; matrix products, arithmetic and copies ran while one was open for 8% -> 0% of each run, Pallas kernels for 0% -> 49%
where the time goes in v2:
time: 141 us
  Pallas kernels  75.2 us (53%)
  waiting for transfers between devices  33.2 us (24%)
  starting transfers between devices  27.8 us (20%)
  local copies, waits for them, and re-layouts  3.22 us (2%)
    pallas_call x3, Pallas kernels, score(): pl.pallas_call(functools.partial(score_kernel, len(rows), sizes, fetch, p...  64.6 us
    ppermute x9, waiting for transfers between devices, move(): return lax.ppermute(value, ('doc', 'cent'), pairs)  27.3 us
    ppermute x9, starting transfers between devices, move(): return lax.ppermute(value, ('doc', 'cent'), pairs)  13.9 us
    all_to_all x1, starting transfers between devices, per_device(): lax.all_to_all(send.reshape(devices, cap, width + ID_LANES), ('doc', 'cen...  8.75 us
    pallas_call x1, Pallas kernels, prepare(): pl.pallas_call(functools.partial(prepare_kernel, per_owner, cap), out_sha...  6.3 us
    all_to_all x1, waiting for transfers between devices, per_device(): lax.all_to_all(send.reshape(devices, cap, width + ID_LANES), ('doc', 'cen...  5.91 us
    all_to_all x1, starting transfers between devices, per_device(): lax.all_to_all(best, ('doc', 'cent'), split_axis=0, concat_axis=0, tiled=...  5.15 us
    pallas_call x1, Pallas kernels, owner_best(): pl.pallas_call(owner_kernel, out_shape=jax.ShapeDtypeStruct((total // cap...  3.41 us
  transfers between devices with their start and end apart: 11, of which 6 were waited for; matrix products, arithmetic and copies ran while one was open for 0% of the time, Pallas kernels for 49%

profile of v2, /device:TPU:0, one launch (start us, length us, event | category | flops | bytes accessed | tf_op | source)
XLA Modules:
  0.0 140.9 jit_solution(14055751294487705438)
XLA Ops:
  0.6 6.3 %prepare.1 = (bf16[512,1024]{1,0:T(8,128)(2,1)}, bf16[1024,1152]{1,0:T(8,128)(2,1)}, bf16[1024,1024]{1,0:T(8,128)(2,1)}) custom-call(f32[512,1024]{1,0:T(8,128)} %refs_0_.1, f32[1024,1024]{1,0:T(8,128)} %refs_1_.1, s32[1,512]{1,0:T(1,128)} %bitcast.12, s32[1,512]{1,0:T(1,128)} %bitcast.14), custom_call_target="tpu_custom_call" | custom-call | flops 1 | bytes 1 | tf_op jit(solution)/shard_map/prepare/pallas_call | solution.py:103
  6.9 0.1 collective-permute-start
  7.0 1.6 %collective-permute-start.3 = (bf16[1024,1024]{1,0:T(8,128)(2,1)}, bf16[1024,1024]{1,0:T(8,128)(2,1)}, u32[]{:S(2)}, u32[]{:S(2)}) collective-permute-start(bf16[1024,1024]{1,0:T(8,128)(2,1)} %get-tuple-element.15.refs_1_.refs_5_), channel_id=1, source_target_pairs={{0,2},{1,19},{4,6},{5,23},{8,10},{9,27},{12,14},{13,31},{2,16},{3,... | collective-permute-start | bytes 6291464 | tf_op jit(solution)/shard_map/ppermute | solution.py:340
  8.7 1.9 %collective-permute-start.1 = (bf16[512,1024]{1,0:T(8,128)(2,1)}, bf16[512,1024]{1,0:T(8,128)(2,1)}, u32[]{:S(2)}, u32[]{:S(2)}) collective-permute-start(bf16[512,1024]{1,0:T(8,128)(2,1)} %get-tuple-element.14.refs_0_), channel_id=1, source_target_pairs={{0,4},{1,13},{4,8},{5,1},{8,12},{9,5},{12,0},{13,9},{2,6},{3,15},{... | collective-permute-start | bytes 3145736 | tf_op jit(solution)/shard_map/ppermute | solution.py:340
  10.6 2.1 %collective-permute-start.2 = (bf16[512,1024]{1,0:T(8,128)(2,1)}, bf16[512,1024]{1,0:T(8,128)(2,1)}, u32[]{:S(2)}, u32[]{:S(2)}) collective-permute-start(bf16[512,1024]{1,0:T(8,128)(2,1)} %get-tuple-element.14.refs_0_), channel_id=1, source_target_pairs={{0,12},{1,5},{4,0},{5,9},{8,4},{9,13},{12,8},{13,1},{2,14},{3,7},{... | collective-permute-start | bytes 3145736 | tf_op jit(solution)/shard_map/ppermute | solution.py:340
  12.7 0.0 copy-start.2
  12.7 8.8 %all-to-all-start = ((bf16[128,8,1152]{2,1,0:T(8,128)(2,1)}), bf16[128,8,1152]{2,1,0:T(8,128)(2,1)S(1)}, u32[]{:S(2)}, u32[]{:S(2)}) async-start(bf16[128,8,1152]{2,1,0:T(8,128)(2,1)} %bitcast.16), calls=%async_computation | async-start | bytes 4718592 | tf_op jit(solution)/shard_map/all_to_all | solution.py:370
  21.5 0.0 collective-permute-done.refs_2_.refs_6_
  21.5 0.0 copy-done.2
  21.5 0.0 copy-start
  21.5 1.6 %copy-done = bf16[1024,1024]{1,0:T(8,128)(2,1)S(1)} copy-done((bf16[1024,1024]{1,0:T(8,128)(2,1)S(1)}, bf16[1024,1024]{1,0:T(8,128)(2,1)}, u32[]{:S(2)}) %copy-start) | copy-done | bytes 2097176
  23.1 10.0 %score_own.1 = (f32[1,512]{1,0:T(1,128)S(1)}, bf16[2048,1024]{1,0:T(8,128)(2,1)}) custom-call(bf16[512,1024]{1,0:T(8,128)(2,1)S(1)} %copy-done.2, bf16[1024,1024]{1,0:T(8,128)(2,1)S(1)} %copy-done, bf16[1024,1024]{1,0:T(8,128)(2,1)} %collective-permute-done.refs_2_.refs_6_), custom_call_target="tpu_custom_call" | custom-call | flops 1 | bytes 1 | tf_op jit(solution)/shard_map/score_own/pallas_call | solution.py:218
  33.1 12.9 %collective-permute-done.1.refs_1_ = bf16[512,1024]{1,0:T(8,128)(2,1)} collective-permute-done((bf16[512,1024]{1,0:T(8,128)(2,1)}, bf16[512,1024]{1,0:T(8,128)(2,1)}, u32[]{:S(2)}, u32[]{:S(2)}) %collective-permute-start.1) | collective-permute-done | bytes 1048608 | tf_op jit(solution)/shard_map/ppermute | solution.py:340
  46.1 0.2 collective-permute-done.3.refs_3_
  46.3 11.3 %collective-permute-done.2.refs_2_ = bf16[512,1024]{1,0:T(8,128)(2,1)} collective-permute-done((bf16[512,1024]{1,0:T(8,128)(2,1)}, bf16[512,1024]{1,0:T(8,128)(2,1)}, u32[]{:S(2)}, u32[]{:S(2)}) %collective-permute-start.2) | collective-permute-done | bytes 1048608 | tf_op jit(solution)/shard_map/ppermute | solution.py:340
  57.6 3.4 %collective-permute-start.4 = (bf16[1024,1024]{1,0:T(8,128)(2,1)}, bf16[1024,1024]{1,0:T(8,128)(2,1)}, u32[]{:S(2)}, u32[]{:S(2)}) collective-permute-start(bf16[1024,1024]{1,0:T(8,128)(2,1)} %collective-permute-done.3.refs_3_), channel_id=1, source_target_pairs={{0,1},{1,0},{4,5},{5,4},{8,9},{9,8},{12,13},{13,12},{2,3},{3,2},{6... | collective-permute-start | bytes 6291464 | tf_op jit(solution)/shard_map/ppermute | solution.py:340
  61.0 0.0 collective-permute-start.7
  61.0 5.9 %all-to-all-done = bf16[128,8,1152]{2,1,0:T(8,128)(2,1)S(1)} async-done(((bf16[128,8,1152]{2,1,0:T(8,128)(2,1)}), bf16[128,8,1152]{2,1,0:T(8,128)(2,1)S(1)}, u32[]{:S(2)}, u32[]{:S(2)}) %all-to-all-start) | async-done | bytes 2359328 | tf_op jit(solution)/shard_map/all_to_all | solution.py:370
  66.9 3.4 %owner_best.1 = f32[128,8]{1,0:T(8,128)} custom-call(bf16[1024,1152]{1,0:T(8,128)(2,1)S(1)} %bitcast.10), custom_call_target="tpu_custom_call" | custom-call | flops 1 | bytes 1 | tf_op jit(solution)/shard_map/owner_best/pallas_call | solution.py:284
  70.4 5.1 %all-to-all-start.1 = ((f32[128,1,8]{2,1,0:T(1,128)}), f32[128,1,8]{2,1,0:T(1,128)S(1)}, u32[]{:S(2)}, u32[]{:S(2)}) async-start(f32[128,1,8]{2,1,0:T(1,128)} %bitcast.6), calls=%async_computation.1 | async-start | bytes 131072 | tf_op jit(solution)/shard_map/all_to_all | solution.py:381
  75.5 0.0 collective-permute-done.4.refs_4_
  75.5 0.0 copy-start.1
  75.5 1.6 %copy-done.1 = bf16[1024,1024]{1,0:T(8,128)(2,1)S(1)} copy-done((bf16[1024,1024]{1,0:T(8,128)(2,1)S(1)}, bf16[1024,1024]{1,0:T(8,128)(2,1)}, u32[]{:S(2)}) %copy-start.1) | copy-done | bytes 2097176
  77.1 38.7 %score_near.1 = (f32[1,1536]{1,0:T(1,128)S(1)}, bf16[4096,1024]{1,0:T(8,128)(2,1)S(1)}) custom-call(bf16[512,1024]{1,0:T(8,128)(2,1)S(1)} %copy-done.2, bf16[512,1024]{1,0:T(8,128)(2,1)} %collective-permute-done.1.refs_1_, bf16[512,1024]{1,0:T(8,128)(2,1)} %collective-permute-done.2.refs_2_, bf16[1024,1024]{1,0:T(8,128)(2,1)} %collective-permute-done.3.refs_3_, ...), custom_call_target="tpu_custom_call" | custom-call | flops 1 | bytes 1 | tf_op jit(solution)/shard_map/score_near/pallas_call | solution.py:218
  115.9 0.0 collective-permute-done.7.refs_0_
  115.9 0.0 copy-start.3
  115.9 0.0 copy-start.4
  115.9 15.8 %score_far.1 = f32[1,512]{1,0:T(1,128)S(1)} custom-call(bf16[512,1024]{1,0:T(8,128)(2,1)} %collective-permute-done.7.refs_0_, bf16[4096,1024]{1,0:T(8,128)(2,1)S(1)} %get-tuple-element.25.refs_1_), custom_call_target="tpu_custom_call" | custom-call | flops 1 | bytes 1 | tf_op jit(solution)/shard_map/score_far/pallas_call | solution.py:218
  131.8 2.7 %collective-permute-start.8 = (f32[1,512]{1,0:T(1,128)S(1)}, f32[1,512]{1,0:T(1,128)S(1)}, u32[]{:S(2)}, u32[]{:S(2)}) collective-permute-start(f32[1,512]{1,0:T(1,128)S(1)} %score_far.1), channel_id=1, source_target_pairs={{0,8},{1,9},{4,12},{5,13},{8,0},{9,1},{12,4},{13,5},{2,10},{3,11},... | collective-permute-start | bytes 6152 | tf_op jit(solution)/shard_map/ppermute | solution.py:340
  134.5 1.0 collective-permute-start.5
  135.4 1.1 collective-permute-start.6
  136.5 0.0 all-to-all-done.1
  136.5 0.0 copy-done.3
  136.5 0.0 copy-done.4
  136.5 0.9 pick.1
  137.4 0.0 collective-permute-done.8
  137.4 0.7 collective-permute-done.5
  138.1 2.2 %collective-permute-done.6 = f32[1,512]{1,0:T(1,128)S(1)} collective-permute-done((f32[1,512]{1,0:T(1,128)S(1)}, f32[1,512]{1,0:T(1,128)S(1)}, u32[]{:S(2)}, u32[]{:S(2)}) %collective-permute-start.6) | collective-permute-done | bytes 2080 | tf_op jit(solution)/shard_map/ppermute | solution.py:340
  140.3 0.6 multiply_subtract_fusion
  (4 shorter events, 0.1 us)
Async XLA Ops:
  6.9 14.5 %collective-permute-start = (bf16[1024,1024]{1,0:T(8,128)(2,1)}, bf16[1024,1024]{1,0:T(8,128)(2,1)}, u32[]{:S(2)}, u32[]{:S(2)}) collective-permute-start(bf16[1024,1024]{1,0:T(8,128)(2,1)} %get-tuple-element.15.refs_1_.refs_5_), channel_id=1, source_target_pairs={{0,1},{1,0},{4,5},{5,4},{8,9},{9,8},{12,13},{13,12},{2,3},{3,2},{6... | collective-permute-start | bytes 6291464 | tf_op jit(solution)/shard_map/ppermute | solution.py:340
  7.0 39.3 %collective-permute-start.3 = (bf16[1024,1024]{1,0:T(8,128)(2,1)}, bf16[1024,1024]{1,0:T(8,128)(2,1)}, u32[]{:S(2)}, u32[]{:S(2)}) collective-permute-start(bf16[1024,1024]{1,0:T(8,128)(2,1)} %get-tuple-element.15.refs_1_.refs_5_), channel_id=1, source_target_pairs={{0,2},{1,19},{4,6},{5,23},{8,10},{9,27},{12,14},{13,31},{2,16},{3,... | collective-permute-start | bytes 6291464 | tf_op jit(solution)/shard_map/ppermute | solution.py:340
  8.7 37.4 %collective-permute-start.1 = (bf16[512,1024]{1,0:T(8,128)(2,1)}, bf16[512,1024]{1,0:T(8,128)(2,1)}, u32[]{:S(2)}, u32[]{:S(2)}) collective-permute-start(bf16[512,1024]{1,0:T(8,128)(2,1)} %get-tuple-element.14.refs_0_), channel_id=1, source_target_pairs={{0,4},{1,13},{4,8},{5,1},{8,12},{9,5},{12,0},{13,9},{2,6},{3,15},{... | collective-permute-start | bytes 3145736 | tf_op jit(solution)/shard_map/ppermute | solution.py:340
  10.6 47.0 %collective-permute-start.2 = (bf16[512,1024]{1,0:T(8,128)(2,1)}, bf16[512,1024]{1,0:T(8,128)(2,1)}, u32[]{:S(2)}, u32[]{:S(2)}) collective-permute-start(bf16[512,1024]{1,0:T(8,128)(2,1)} %get-tuple-element.14.refs_0_), channel_id=1, source_target_pairs={{0,12},{1,5},{4,0},{5,9},{8,4},{9,13},{12,8},{13,1},{2,14},{3,7},{... | collective-permute-start | bytes 3145736 | tf_op jit(solution)/shard_map/ppermute | solution.py:340
  12.7 8.8 %copy-start.2 = (bf16[512,1024]{1,0:T(8,128)(2,1)S(1)}, bf16[512,1024]{1,0:T(8,128)(2,1)}, u32[]{:S(2)}) copy-start(bf16[512,1024]{1,0:T(8,128)(2,1)} %get-tuple-element.14.refs_0_) | copy-start | bytes 3145732
  12.7 54.2 %all-to-all-start = ((bf16[128,8,1152]{2,1,0:T(8,128)(2,1)}), bf16[128,8,1152]{2,1,0:T(8,128)(2,1)S(1)}, u32[]{:S(2)}, u32[]{:S(2)}) async-start(bf16[128,8,1152]{2,1,0:T(8,128)(2,1)} %bitcast.16), calls=%async_computation | async-start | bytes 4718592 | tf_op jit(solution)/shard_map/all_to_all | solution.py:370
  21.5 1.6 %copy-start = (bf16[1024,1024]{1,0:T(8,128)(2,1)S(1)}, bf16[1024,1024]{1,0:T(8,128)(2,1)}, u32[]{:S(2)}) copy-start(bf16[1024,1024]{1,0:T(8,128)(2,1)} %get-tuple-element.15.refs_1_.refs_5_) | copy-start | bytes 6291460
  57.6 17.9 %collective-permute-start.4 = (bf16[1024,1024]{1,0:T(8,128)(2,1)}, bf16[1024,1024]{1,0:T(8,128)(2,1)}, u32[]{:S(2)}, u32[]{:S(2)}) collective-permute-start(bf16[1024,1024]{1,0:T(8,128)(2,1)} %collective-permute-done.3.refs_3_), channel_id=1, source_target_pairs={{0,1},{1,0},{4,5},{5,4},{8,9},{9,8},{12,13},{13,12},{2,3},{3,2},{6... | collective-permute-start | bytes 6291464 | tf_op jit(solution)/shard_map/ppermute | solution.py:340
  61.0 54.8 %collective-permute-start.7 = (bf16[512,1024]{1,0:T(8,128)(2,1)}, bf16[512,1024]{1,0:T(8,128)(2,1)}, u32[]{:S(2)}, u32[]{:S(2)}) collective-permute-start(bf16[512,1024]{1,0:T(8,128)(2,1)} %collective-permute-done.1.refs_1_), channel_id=1, source_target_pairs={{0,4},{1,13},{4,8},{5,1},{8,12},{9,5},{12,0},{13,9},{2,6},{3,15},{... | collective-permute-start | bytes 3145736 | tf_op jit(solution)/shard_map/ppermute | solution.py:340
  70.4 66.1 %all-to-all-start.1 = ((f32[128,1,8]{2,1,0:T(1,128)}), f32[128,1,8]{2,1,0:T(1,128)S(1)}, u32[]{:S(2)}, u32[]{:S(2)}) async-start(f32[128,1,8]{2,1,0:T(1,128)} %bitcast.6), calls=%async_computation.1 | async-start | bytes 131072 | tf_op jit(solution)/shard_map/all_to_all | solution.py:381
  75.5 1.6 %copy-start.1 = (bf16[1024,1024]{1,0:T(8,128)(2,1)S(1)}, bf16[1024,1024]{1,0:T(8,128)(2,1)}, u32[]{:S(2)}) copy-start(bf16[1024,1024]{1,0:T(8,128)(2,1)} %get-tuple-element.15.refs_1_.refs_5_) | copy-start | bytes 6291460
  115.9 20.6 %copy-start.3 = (s32[512]{0:T(512)S(1)}, s32[512]{0:T(512)}, u32[]{:S(2)}) copy-start(s32[512]{0:T(512)} %param.6) | copy-start | bytes 6148
  115.9 20.6 %copy-start.4 = (s32[512]{0:T(512)S(1)}, s32[512]{0:T(512)}, u32[]{:S(2)}) copy-start(s32[512]{0:T(512)} %param.7) | copy-start | bytes 6148
  131.8 5.6 %collective-permute-start.8 = (f32[1,512]{1,0:T(1,128)S(1)}, f32[1,512]{1,0:T(1,128)S(1)}, u32[]{:S(2)}, u32[]{:S(2)}) collective-permute-start(f32[1,512]{1,0:T(1,128)S(1)} %score_far.1), channel_id=1, source_target_pairs={{0,8},{1,9},{4,12},{5,13},{8,0},{9,1},{12,4},{13,5},{2,10},{3,11},... | collective-permute-start | bytes 6152 | tf_op jit(solution)/shard_map/ppermute | solution.py:340
  134.5 3.6 %collective-permute-start.5 = (f32[1,512]{1,0:T(1,128)S(1)}, f32[1,512]{1,0:T(1,128)S(1)}, u32[]{:S(2)}, u32[]{:S(2)}) collective-permute-start(f32[1,512]{1,0:T(1,128)S(1)} %get-tuple-element.28), channel_id=1, source_target_pairs={{0,12},{1,5},{4,0},{5,9},{8,4},{9,13},{12,8},{13,1},{2,14},{3,7},{... | collective-permute-start | bytes 6152 | tf_op jit(solution)/shard_map/ppermute | solution.py:340
  135.4 4.8 %collective-permute-start.6 = (f32[1,512]{1,0:T(1,128)S(1)}, f32[1,512]{1,0:T(1,128)S(1)}, u32[]{:S(2)}, u32[]{:S(2)}) collective-permute-start(f32[1,512]{1,0:T(1,128)S(1)} %get-tuple-element.29), channel_id=1, source_target_pairs={{0,4},{1,13},{4,8},{5,1},{8,12},{9,5},{12,0},{13,9},{2,6},{3,15},{... | collective-permute-start | bytes 6152 | tf_op jit(solution)/shard_map/ppermute | solution.py:340

commit v3 on v2

--- a/solution.py
+++ b/solution.py
@@ -25,41 +25,38 @@
 STEP = 512
 
 
+def in_hbm(value):
+    return pltpu.with_memory_space_constraint(value, pltpu.HBM)
+
+
 def unit_of(values):
     total = jnp.sum(values * values, axis=1, keepdims=True)
     return (values * lax.rsqrt(total + 1e-06)).astype(jnp.bfloat16)
 
 
-def prepare_kernel(per_owner, cap, *refs):
-    emb_hbm, cen_hbm, cluster_hbm, slot_hbm = refs[:4]
-    unit_hbm, send_hbm, centre_hbm = refs[4:7]
-    emb, cen, cluster_ref, slot_ref, unit_ref, send_ref, centre_ref = refs[7:14]
-    emb_sems, cen_sems, id_sems, unit_sems, send_sems, centre_sems = refs[14:]
+def rows_kernel(per_owner, cap, *refs):
+    emb_hbm, cluster_hbm, slot_hbm, unit_hbm, send_hbm = refs[:5]
+    emb, cluster_ref, slot_ref, unit_ref, send_ref = refs[5:10]
+    emb_sems, id_sems, unit_sems, send_sems = refs[10:]
     rows, width = emb.shape
-
-    def copy_of(src, dst, sem):
-        return pltpu.make_async_copy(src, dst, sem)
 
     def piece(ref, i, size=CHUNK):
         return ref.at[pl.ds(i * size, size)]
 
     ids = [
-        copy_of(cluster_hbm, cluster_ref, id_sems.at[0]),
-        copy_of(slot_hbm, slot_ref, id_sems.at[1]),
+        pltpu.make_async_copy(cluster_hbm, cluster_ref, id_sems.at[0]),
+        pltpu.make_async_copy(slot_hbm, slot_ref, id_sems.at[1]),
     ]
     emb_copies = [
-        copy_of(piece(emb_hbm, i), piece(emb, i), emb_sems.at[i]) for i in range(rows // CHUNK)
-    ]
-    cen_copies = [
-        copy_of(piece(cen_hbm, i), piece(cen, i), cen_sems.at[i])
-        for i in range(cen.shape[0] // CHUNK)
-    ]
-    for copy in emb_copies + ids + cen_copies:
+        pltpu.make_async_copy(piece(emb_hbm, i), piece(emb, i), emb_sems.at[i])
+        for i in range(rows // CHUNK)
+    ]
+    for copy in emb_copies + ids:
         copy.start()
     out = []
 
     def send_out(src, dst, sem):
-        out.append(copy_of(src, dst, sem))
+        out.append(pltpu.make_async_copy(src, dst, sem))
         out[-1].start()
 
     for i, copy in enumerate(emb_copies):
@@ -84,117 +81,171 @@
             lax.dot_general(hot, names, NT, preferred_element_type=jnp.float32) - 1.0
         ).astype(jnp.bfloat16)
         send_out(piece(send_ref, i, LANES), piece(send_hbm, i, LANES), send_sems.at[i])
-    for i, copy in enumerate(cen_copies):
-        copy.wait()
-        part = slice(i * CHUNK, (i + 1) * CHUNK)
-        centre_ref[part] = unit_of(cen[part])
-        send_out(piece(centre_ref, i), piece(centre_hbm, i), centre_sems.at[i])
     for copy in out:
         copy.wait()
 
 
-def prepare(embeddings, centroids, cluster, slot, per_owner, cap, devices):
+def prepare_rows(embeddings, cluster, slot, per_owner, cap, devices):
     rows, width = embeddings.shape
-    count = centroids.shape[0]
     send = (devices * cap, width + ID_LANES)
-    shapes = ((rows, width), send, (count, width))
-    sems = (rows // CHUNK, count // CHUNK, 2, rows // CHUNK, send[0] // LANES)
-    sems += (count // CHUNK,)
     return pl.pallas_call(
-        functools.partial(prepare_kernel, per_owner, cap),
-        out_shape=tuple(jax.ShapeDtypeStruct(shape, jnp.bfloat16) for shape in shapes),
-        in_specs=[ANY] * 4,
-        out_specs=(ANY,) * 3,
+        functools.partial(rows_kernel, per_owner, cap),
+        out_shape=tuple(jax.ShapeDtypeStruct(shape, jnp.bfloat16) for shape in ((rows, width), send)),
+        in_specs=[ANY] * 3,
+        out_specs=(ANY,) * 2,
         scratch_shapes=[
             pltpu.VMEM((rows, width), jnp.float32),
-            pltpu.VMEM((count, width), jnp.float32),
             pltpu.VMEM((1, rows), jnp.int32),
             pltpu.VMEM((1, rows), jnp.int32),
             pltpu.VMEM((rows, width), jnp.bfloat16),
             pltpu.VMEM(send, jnp.bfloat16),
-            pltpu.VMEM((count, width), jnp.bfloat16),
         ]
-        + [pltpu.SemaphoreType.DMA((n,)) for n in sems],
+        + [pltpu.SemaphoreType.DMA((n,)) for n in (rows // CHUNK, 2, rows // CHUNK, send[0] // LANES)],
         compiler_params=PARAMS,
         cost_estimate=TINY,
-        name="prepare",
-    )(embeddings, centroids, cluster.reshape(1, rows), slot.reshape(1, rows))
-
-
-def score_kernel(n_rows, sizes, fetch, plan, *refs):
-    n_cent = len(sizes)
-    row_refs, refs = refs[:n_rows], refs[n_rows:]
-    if fetch:
-        cent_refs, (out_ref, table), refs = refs[:n_cent], refs[n_cent : n_cent + 2], refs[n_cent + 2 :]
-    else:
-        cent_refs, (table, out_ref), refs = (), refs[:2], refs[2:]
-    rows, high, total, row_sems, cent_sems = refs
-
-    def copies_of(arrays, buffer, sems):
-        copies, i, base = [], 0, 0
-        for ref in arrays:
+        name="prepare_rows",
+    )(embeddings, cluster.reshape(1, rows), slot.reshape(1, rows))
+
+
+def centres_kernel(cen_hbm, centre_hbm, cen, centre_ref, in_sems, out_sems):
+    parts = [pl.ds(i * CHUNK, CHUNK) for i in range(cen.shape[0] // CHUNK)]
+    copies = [
+        pltpu.make_async_copy(cen_hbm.at[part], cen.at[part], in_sems.at[i])
+        for i, part in enumerate(parts)
+    ]
+    out = [
+        pltpu.make_async_copy(centre_ref.at[part], centre_hbm.at[part], out_sems.at[i])
+        for i, part in enumerate(parts)
+    ]
+    for copy in copies:
+        copy.start()
+    for i, part in enumerate(parts):
+        copies[i].wait()
+        centre_ref[part] = unit_of(cen[part])
+        out[i].start()
+    for copy in out:
+        copy.wait()
+
+
+def prepare_centres(centroids):
+    count, width = centroids.shape
+    return pl.pallas_call(
+        centres_kernel,
+        out_shape=jax.ShapeDtypeStruct((count, width), jnp.bfloat16),
+        in_specs=[ANY],
+        out_specs=ANY,
+        scratch_shapes=[
+            pltpu.VMEM((count, width), jnp.float32),
+            pltpu.VMEM((count, width), jnp.bfloat16),
+            pltpu.SemaphoreType.DMA((count // CHUNK,)),
+            pltpu.SemaphoreType.DMA((count // CHUNK,)),
+        ],
+        compiler_params=PARAMS,
+        cost_estimate=TINY,
+        name="prepare_centres",
+    )(centroids)
+
+
+def score_kernel(rows_new, rows_kept, cents_new, cents_kept, priors, plan, keep, *refs):
+    refs = list(refs)
+
+    def take(n):
+        head = refs[:n]
+        del refs[:n]
+        return head
+
+    row_refs, cent_refs = take(len(rows_new)), take(len(cents_new))
+    (kept_rows,) = take(1) if rows_kept else (None,)
+    (kept_cents,) = take(1) if cents_kept else (None,)
+    (prior_ref,) = take(1)
+    (out_ref,) = take(1)
+    rows, table, high, total, row_sems, cent_sems = refs
+
+    def places(new, kept, buffer, kept_buffer):
+        sources = [(buffer, sum(new[:i]), size) for i, size in enumerate(new)]
+        return sources + [(kept_buffer, sum(kept[:i]), size) for i, size in enumerate(kept)]
+
+    row_at = places(rows_new, rows_kept, rows, kept_rows)
+    cent_at = places(cents_new, cents_kept, table, kept_cents)
+    lane_at = [sum(size for _, _, size in row_at[:j]) for j in range(len(row_at))]
+
+    def copies_of(arrays, sizes, buffer, sems):
+        copies, i = [], 0
+        for k, ref in enumerate(arrays):
             mine = []
-            size = min(STEP, ref.shape[0])
-            for start in range(0, ref.shape[0], size):
+            for start in range(0, sizes[k], STEP):
+                place = pl.ds(sum(sizes[:k]) + start, STEP)
                 mine.append(
-                    pltpu.make_async_copy(
-                        ref.at[pl.ds(start, size)], buffer.at[pl.ds(base + start, size)], sems.at[i]
-                    )
+                    pltpu.make_async_copy(ref.at[pl.ds(start, STEP)], buffer.at[place], sems.at[i])
                 )
                 i += 1
             copies.append(mine)
-            base += ref.shape[0]
         return copies
 
-    row_starts = [sum(ref.shape[0] for ref in row_refs[:j]) for j in range(n_rows)]
-    cent_starts = [sum(sizes[:i]) for i in range(n_cent)]
-    row_copies = copies_of(row_refs, rows, row_sems)
-    cent_copies = copies_of(cent_refs, table, cent_sems)
+    row_copies = copies_of(row_refs, rows_new, rows, row_sems)
+    cent_copies = copies_of(cent_refs, cents_new, table, cent_sems)
     stages = [
         [copy for j in new_rows for copy in row_copies[j]]
-        + [copy for i in new_cents if fetch for copy in cent_copies[i]]
+        + [copy for i in new_cents for copy in cent_copies[i]]
         for new_rows, new_cents, _ in plan
     ]
 
-    def product(cent, lanes):
-        return lax.dot_general(
-            table[pl.ds(cent, STEP)], rows[lanes], NT, preferred_element_type=jnp.float32
+    def product(i, j, cent, row):
+        cents, cent_start, _ = cent_at[i]
+        values, row_start, _ = row_at[j]
+        return SCALE * lax.dot_general(
+            cents[pl.ds(cent_start + cent, STEP)],
+            values[pl.ds(row_start + row, LANES)],
+            NT,
+            preferred_element_type=jnp.float32,
         )
+
+    def begin():
+        base = 0
+        for j, (_, _, size) in enumerate(row_at):
+            lanes = slice(lane_at[j], lane_at[j] + size)
+            if j in priors:
+                first = lax.broadcasted_iota(jnp.int32, (8, size), 0) == 0
+                high[:, lanes] = jnp.broadcast_to(prior_ref[:, base : base + size], (8, size))
+                total[:, lanes] = jnp.where(first, 1.0, 0.0)
+                base += size
+            else:
+                high[:, lanes] = jnp.full((8, size), -1e30, jnp.float32)
+                total[:, lanes] = jnp.zeros((8, size), jnp.float32)
 
     for copy in stages[0]:
         copy.start()
-    begun = set()
+    begin()
+    begun = set(priors)
     for k, (_, _, products) in enumerate(plan):
         for copy in stages[k]:
             copy.wait()
         for copy in stages[k + 1] if k + 1 < len(plan) else []:
             copy.start()
         for i, j in products:
-            for row in range(row_starts[j], row_starts[j] + row_refs[j].shape[0], LANES):
-                lanes = slice(row, row + LANES)
-                for cent in range(cent_starts[i], cent_starts[i] + sizes[i], STEP):
-                    value = product(cent, lanes) * SCALE
-                    if row not in begun:
+            for row in range(0, row_at[j][2], LANES):
+                lanes = slice(lane_at[j] + row, lane_at[j] + row + LANES)
+                for cent in range(0, cent_at[i][2], STEP):
+                    value = product(i, j, cent, row)
+                    if j not in begun and cent == 0:
                         shift = jnp.max(value, axis=0, keepdims=True)
                         high[:, lanes] = jnp.broadcast_to(shift, (8, LANES))
                     value = jnp.exp2(value.reshape(STEP // 8, 8, LANES) - high[:, lanes][None])
-                    value = jnp.sum(value, axis=0)
-                    total[:, lanes] = value if row not in begun else total[:, lanes] + value
-                    begun.add(row)
+                    total[:, lanes] += jnp.sum(value, axis=0)
+            begun.add(j)
 
     @pl.when(jnp.logical_not(jnp.max(total[...]) < 1e38))
     def _():
-        high[...] = jnp.full_like(high, -1e30)
-        total[...] = jnp.zeros_like(total)
+        begin()
         for i, j in [pair for _, _, products in plan for pair in products]:
 
-            @pl.loop(0, row_refs[j].shape[0] // LANES)
+            @pl.loop(0, row_at[j][2] // LANES)
             def _(r):
-                @pl.loop(0, sizes[i] // STEP)
+                @pl.loop(0, cent_at[i][2] // STEP)
                 def _(c):
-                    lanes = pl.ds(pl.multiple_of(row_starts[j] + r * LANES, LANES), LANES)
-                    value = product(pl.multiple_of(cent_starts[i] + c * STEP, STEP), lanes) * SCALE
-                    value = value.reshape(STEP // 8, 8, LANES)
+                    lanes = pl.ds(pl.multiple_of(lane_at[j] + r * LANES, LANES), LANES)
+                    row, cent = pl.multiple_of(r * LANES, LANES), pl.multiple_of(c * STEP, STEP)
+                    value = product(i, j, cent, row).reshape(STEP // 8, 8, LANES)
                     before = high[:, lanes]
                     now = jnp.maximum(before, jnp.max(value, axis=0))
                     high[:, lanes] = now
@@ -207,30 +258,37 @@
     out_ref[...] = top + jnp.log2(all_sum)
 
 
-def score(rows, centres, plan, name, sizes=None):
-    fetch = sizes is None
-    if fetch:
-        sizes = tuple(value.shape[0] for value in centres)
-    width = rows[0].shape[1]
-    count = sum(value.shape[0] for value in rows)
+def score(rows, centres, plan, name, vmem, prior=None, priors=(), kept=None, keep=False):
+    width = (*rows, *centres)[0].shape[1]
+    rows_new = tuple(value.shape[0] for value in rows)
+    cents_new = tuple(value.shape[0] for value in centres)
+    kept_rows, rows_kept, kept_cents, cents_kept = kept or (None, (), None, ())
+    count = sum(rows_new) + sum(rows_kept)
     out = jax.ShapeDtypeStruct((1, count), jnp.float32)
-    table = jax.ShapeDtypeStruct((sum(sizes), width), jnp.bfloat16)
+    held = [(sum(rows_new) or 16, width), (sum(cents_new) or 16, width)]
+    resident = [value for value in (kept_rows, kept_cents) if value is not None]
+    if prior is None:
+        prior = jnp.zeros((1, 128), jnp.float32)
     return pl.pallas_call(
-        functools.partial(score_kernel, len(rows), sizes, fetch, plan),
-        out_shape=(out, table) if fetch else out,
-        in_specs=[ANY] * len(rows) + ([ANY] * len(centres) if fetch else [VMEM]),
-        out_specs=(VMEM, VMEM) if fetch else VMEM,
-        scratch_shapes=[
-            pltpu.VMEM((count, width), jnp.bfloat16),
+        functools.partial(
+            score_kernel, rows_new, rows_kept, cents_new, cents_kept, tuple(priors), plan, keep
+        ),
+        out_shape=(out, *[jax.ShapeDtypeStruct(shape, jnp.bfloat16) for shape in held])
+        if keep
+        else out,
+        in_specs=[ANY] * (len(rows) + len(centres)) + [VMEM] * (len(resident) + 1),
+        out_specs=(VMEM,) * 3 if keep else VMEM,
+        scratch_shapes=([] if keep else [pltpu.VMEM(shape, jnp.bfloat16) for shape in held])
+        + [
             pltpu.VMEM((8, count), jnp.float32),
             pltpu.VMEM((8, count), jnp.float32),
-            pltpu.SemaphoreType.DMA((count // LANES,)),
-            pltpu.SemaphoreType.DMA((sum(sizes) // STEP,)),
+            pltpu.SemaphoreType.DMA((sum(rows_new) // STEP or 1,)),
+            pltpu.SemaphoreType.DMA((sum(cents_new) // STEP,)),
         ],
-        compiler_params=SCORE_PARAMS,
-        cost_estimate=TINY,
+        compiler_params=pltpu.CompilerParams(vmem_limit_bytes=vmem * 1024 * 1024),
+        cost_estimate=pl.CostEstimate(flops=1 if name == "score_far" else 1, bytes_accessed=1, transcendentals=0),
         name=name,
-    )(*rows, *(centres if fetch else (centres,)))
+    )(*(map(in_hbm, (*rows, *centres)) if kept is None else (*rows, *centres)), *resident, prior)
 
 
 def owner_kernel(rows_hbm, out_ref, rows_ref, sems):
@@ -358,11 +416,12 @@
     per_owner = centroids.shape[0] // lax.axis_size("doc")
     cap = 2 * row_count // devices
 
-    unit, send, centre = prepare(embeddings, centroids, cluster, slot, per_owner, cap, devices)
+    unit, send = prepare_rows(embeddings, cluster, slot, per_owner, cap, devices)
+    centre = prepare_centres(lax.optimization_barrier((centroids, unit))[0])
     ahead, behind = move_z(unit, 1), move_z(unit, -1)
     side, core = move_x(centre), swap_core(centre)
     plan = (((0,), (0,), ((0, 0),)), ((), (1,), ((1, 0),)))
-    first, _ = score((unit,), (centre, core), plan, "score_own")
+    first = score((unit,), (centre, core), plan, "score_own", 24)
 
     def after(value, done):
         return lax.optimization_barrier((value, done))[0]
@@ -374,29 +433,41 @@
         concat_axis=0,
         tiled=True,
     )
-    side, ahead, behind = after(side, first), after(ahead, first), after(behind, first)
+    best = owner_best(after(got, first).reshape(devices * cap, width + ID_LANES), cap)
+    returned = lax.all_to_all(best, ("doc", "cent"), split_axis=0, concat_axis=0, tiled=True)
+
+    side, ahead, behind = after(side, returned), after(ahead, returned), after(behind, returned)
     side_core = swap_core(after(side, (ahead, behind)))
     far = move_z(ahead, 1)
-    best = owner_best(after(got, first).reshape(devices * cap, width + ID_LANES), cap)
-    returned = lax.all_to_all(best, ("doc", "cent"), split_axis=0, concat_axis=0, tiled=True)
-
-    centres = (side, side_core, centre, core)
     plan = (
         ((0, 1), (0,), ((0, 0), (0, 1))),
-        ((2,), (1,), ((1, 0), (1, 1), (0, 2), (1, 2))),
-        ((), (2, 3), ((2, 1), (2, 2), (3, 1), (3, 2))),
-    )
-    near, table = score((unit, ahead, after(behind, best)), centres, plan, "score_near")
-    parts = [near[:, i * row_count : (i + 1) * row_count] for i in range(3)]
-    plan = (((0,), (0, 1, 2, 3), ((0, 0), (1, 0), (2, 0), (3, 0))),)
-    sizes = tuple(value.shape[0] for value in centres)
-    last = score((far,), table, plan, "score_far", sizes)
-
-    terms = (first, parts[0], move_z(parts[1], -1), move_z(parts[2], 1))
-    terms = jnp.concatenate([*terms, move_z(last, 2)], axis=0)
+        ((2,), (1,), ((0, 2), (1, 1), (1, 2))),
+        ((), (2,), ((2, 1), (2, 2))),
+    )
+    near, rows, table = score(
+        (unit, ahead, behind),
+        (side, centre, core),
+        plan,
+        "score_near",
+        24,
+        prior=first,
+        priors=(0,),
+        keep=True,
+    )
+    plan = (((), (0,), ((0, 0), (0, 1), (0, 2))),)
+    sizes = (row_count,) * 3
+    mid = score(
+        (), (side_core,), plan, "score_mid", 16, prior=near, priors=(0, 1, 2), kept=(rows, sizes, None, ())
+    )
+    parts = [mid[:, i * row_count : (i + 1) * row_count] for i in range(3)]
+    dup_sim = pick(after(returned, near), cluster, slot, per_owner)
+    plan = (((0,), (), ((1, 0), (2, 0), (3, 0))), ((), (0,), ((0, 0),)))
+    kept = (None, (), table, (centre.shape[0],) * 3)
+    last = score((after(far, (mid, dup_sim)),), (side_core,), plan, "score_far", 16, kept=kept)
+    terms = (move_z(last, 2), parts[0], move_z(parts[1], -1), move_z(parts[2], 1))
+    terms = jnp.concatenate(terms, axis=0)
     top = jnp.max(terms, axis=0)
     soft_cost = 1.0 - BACK * (top + jnp.log2(jnp.sum(jnp.exp2(terms - top[None]), axis=0)))
-    dup_sim = pick(returned, cluster, slot, per_owner)
     return (soft_cost, dup_sim)
 
 

time: 141 us -> 138 us (0.979)
  starting transfers between devices: 27.8 us -> 24.9 us
  local copies, waits for them, and re-layouts: 3.22 us -> 1.41 us
    ppermute x9, waiting for transfers between devices: 27.3 us -> 14 us  [move(): return lax.ppermute(value, ('doc', 'cent'), pairs)]
    all_to_all x1, waiting for transfers between devices: 5.91 us -> 14.2 us  [per_device(): lax.all_to_all(send.reshape(devices, cap, width + ID_LANES), ('doc', 'cen...]
    all_to_all x1, waiting for transfers between devices: 0.01 us -> 5.81 us  [per_device(): lax.all_to_all(best, ('doc', 'cent'), split_axis=0, concat_axis=0, tiled=...]
    ppermute x9, starting transfers between devices: 13.9 us -> 9.09 us  [move(): return lax.ppermute(value, ('doc', 'cent'), pairs)]
    all_to_all x1, starting transfers between devices: 8.75 us -> 11.1 us  [per_device(): lax.all_to_all(send.reshape(devices, cap, width + ID_LANES), ('doc', 'cen...]
    unnamed x10 -> x8, local copies, waits for them, and re-layouts: 3.18 us -> 1.4 us
    pallas_call x4 -> x6, Pallas kernels: 70.9 us -> 71.4 us  [the longest x4 64 us: score(): pl.pallas_call(functools.partial(score_kernel, rows_new, rows_kept, cents...]
  transfers between devices with their start and end apart: 11 -> 11, of which waited for: 6 -> 5; matrix products, arithmetic and copies ran while one was open for 0% -> 0% of each run, Pallas kernels for 49% -> 41%
where the time goes in v3:
time: 138 us; the launch traced here: 137 us
  Pallas kernels  75.7 us (55%)
  waiting for transfers between devices  34 us (25%)
  starting transfers between devices  24.9 us (18%)
  local copies, waits for them, and re-layouts  1.41 us (1%)
    pallas_call x4, Pallas kernels, score(): pl.pallas_call(functools.partial(score_kernel, rows_new, rows_kept, cents...  64 us
    all_to_all x1, waiting for transfers between devices, per_device(): lax.all_to_all(send.reshape(devices, cap, width + ID_LANES), ('doc', 'cen...  14.2 us
    ppermute x9, waiting for transfers between devices, move(): return lax.ppermute(value, ('doc', 'cent'), pairs)  14 us
    all_to_all x1, starting transfers between devices, per_device(): lax.all_to_all(send.reshape(devices, cap, width + ID_LANES), ('doc', 'cen...  11.1 us
    ppermute x9, starting transfers between devices, move(): return lax.ppermute(value, ('doc', 'cent'), pairs)  9.09 us
    all_to_all x1, waiting for transfers between devices, per_device(): lax.all_to_all(best, ('doc', 'cent'), split_axis=0, concat_axis=0, tiled=...  5.81 us
    all_to_all x1, starting transfers between devices, per_device(): lax.all_to_all(best, ('doc', 'cent'), split_axis=0, concat_axis=0, tiled=...  4.62 us
    pallas_call x1, Pallas kernels, prepare_rows(): pl.pallas_call(functools.partial(rows_kernel, per_owner, cap), out_shape=...  4.14 us
  transfers between devices with their start and end apart: 11, of which 5 were waited for; matrix products, arithmetic and copies ran while one was open for 0% of the time, Pallas kernels for 41%

profile of v3, /device:TPU:0, one launch (start us, length us, event | category | flops | bytes accessed | tf_op | source)
XLA Modules:
  0.0 137.4 jit_solution(7335504363540541158)
XLA Ops:
  0.6 4.1 %prepare_rows.1 = (bf16[512,1024]{1,0:T(8,128)(2,1)}, bf16[1024,1152]{1,0:T(8,128)(2,1)}) custom-call(f32[512,1024]{1,0:T(8,128)} %refs_0_.1, s32[1,512]{1,0:T(1,128)} %bitcast.12, s32[1,512]{1,0:T(1,128)} %bitcast.14), custom_call_target="tpu_custom_call" | custom-call | flops 1 | bytes 1 | tf_op jit(solution)/shard_map/prepare_rows/pallas_call | solution.py:91
  4.8 11.1 %all-to-all-start = ((bf16[128,8,1152]{2,1,0:T(8,128)(2,1)}), bf16[128,8,1152]{2,1,0:T(8,128)(2,1)S(1)}, u32[]{:S(2)}, u32[]{:S(2)}) async-start(bf16[128,8,1152]{2,1,0:T(8,128)(2,1)} %bitcast.16), calls=%async_computation | async-start | bytes 4718592 | tf_op jit(solution)/shard_map/all_to_all | solution.py:429
  15.9 0.0 copy-start.3
  15.9 3.3 %prepare_centres.1.refs_1_.refs_4_ = bf16[1024,1024]{1,0:T(8,128)(2,1)} custom-call(f32[1024,1024]{1,0:T(8,128)} %cen_hbm), custom_call_target="tpu_custom_call" | custom-call | flops 1 | bytes 1 | tf_op jit(solution)/shard_map/prepare_centres/pallas_call | solution.py:132
  19.3 0.1 collective-permute-start.1
  19.4 1.1 collective-permute-start.3
  20.5 0.0 copy-done.3
  20.5 1.6 %collective-permute-start = (bf16[512,1024]{1,0:T(8,128)(2,1)S(1)}, bf16[512,1024]{1,0:T(8,128)(2,1)}, u32[]{:S(2)}, u32[]{:S(2)}) collective-permute-start(bf16[512,1024]{1,0:T(8,128)(2,1)S(1)} %copy-done.3), channel_id=1, source_target_pairs={{0,4},{1,13},{4,8},{5,1},{8,12},{9,5},{12,0},{13,9},{2,6},{3,15},{... | collective-permute-start | bytes 3145736 | tf_op jit(solution)/shard_map/ppermute | solution.py:398
  22.1 1.8 %collective-permute-start.4 = (bf16[512,1024]{1,0:T(8,128)(2,1)S(1)}, bf16[512,1024]{1,0:T(8,128)(2,1)}, u32[]{:S(2)}, u32[]{:S(2)}) collective-permute-start(bf16[512,1024]{1,0:T(8,128)(2,1)S(1)} %copy-done.3), channel_id=1, source_target_pairs={{0,12},{1,5},{4,0},{5,9},{8,4},{9,13},{12,8},{13,1},{2,14},{3,7},{... | collective-permute-start | bytes 3145736 | tf_op jit(solution)/shard_map/ppermute | solution.py:398
  23.8 0.0 collective-permute-done.1.refs_2_.refs_5_
  23.8 0.0 copy-start.2
  23.8 1.4 %copy-done.2 = bf16[1024,1024]{1,0:T(8,128)(2,1)} copy-done((bf16[1024,1024]{1,0:T(8,128)(2,1)}, bf16[1024,1024]{1,0:T(8,128)(2,1)S(1)}, u32[]{:S(2)}) %copy-start.2) | copy-done | bytes 2097176
  25.2 9.7 %score_own.1.refs_6_ = f32[1,512]{1,0:T(1,128)S(1)} custom-call(bf16[512,1024]{1,0:T(8,128)(2,1)} %get-tuple-element.15.refs_0_, bf16[1024,1024]{1,0:T(8,128)(2,1)} %prepare_centres.1.refs_1_.refs_4_, bf16[1024,1024]{1,0:T(8,128)(2,1)} %copy-done.2, f32[1,128]{1,0:T(1,128)S(1)} %broadcast_1_refs_3_.2.refs_3_), custom_call_target="tpu_custom_call" | custom-call | flops 1 | bytes 1 | tf_op jit(solution)/shard_map/score_own/pallas_call | solution.py:272
  35.0 14.2 %all-to-all-done = bf16[128,8,1152]{2,1,0:T(8,128)(2,1)S(1)} async-done(((bf16[128,8,1152]{2,1,0:T(8,128)(2,1)}), bf16[128,8,1152]{2,1,0:T(8,128)(2,1)S(1)}, u32[]{:S(2)}, u32[]{:S(2)}) %all-to-all-start) | async-done | bytes 2359328 | tf_op jit(solution)/shard_map/all_to_all | solution.py:429
  49.2 3.4 %owner_best.1 = f32[128,8]{1,0:T(8,128)} custom-call(bf16[1024,1152]{1,0:T(8,128)(2,1)S(1)} %bitcast.10), custom_call_target="tpu_custom_call" | custom-call | flops 1 | bytes 1 | tf_op jit(solution)/shard_map/owner_best/pallas_call | solution.py:342
  52.6 4.6 %all-to-all-start.1 = ((f32[128,1,8]{2,1,0:T(1,128)}), f32[128,1,8]{2,1,0:T(1,128)S(1)}, u32[]{:S(2)}, u32[]{:S(2)}) async-start(f32[128,1,8]{2,1,0:T(1,128)} %bitcast.5), calls=%async_computation.1 | async-start | bytes 131072 | tf_op jit(solution)/shard_map/all_to_all | solution.py:437
  57.2 9.4 %collective-permute-done.3.refs_3_ = bf16[1024,1024]{1,0:T(8,128)(2,1)} collective-permute-done((bf16[1024,1024]{1,0:T(8,128)(2,1)}, bf16[1024,1024]{1,0:T(8,128)(2,1)}, u32[]{:S(2)}, u32[]{:S(2)}) %collective-permute-start.3) | collective-permute-done | bytes 2097184 | tf_op jit(solution)/shard_map/ppermute | solution.py:398
  66.6 5.8 %all-to-all-done.1 = f32[128,1,8]{2,1,0:T(1,128)S(1)} async-done(((f32[128,1,8]{2,1,0:T(1,128)}), f32[128,1,8]{2,1,0:T(1,128)S(1)}, u32[]{:S(2)}, u32[]{:S(2)}) %all-to-all-start.1) | async-done | bytes 4128 | tf_op jit(solution)/shard_map/all_to_all | solution.py:437
  72.5 0.0 copy-start
  72.5 0.0 copy-start.1
  72.5 0.0 collective-permute-done.refs_1_
  72.5 0.0 collective-permute-done.4.refs_2_
  72.5 0.1 collective-permute-start.5
  72.6 1.1 collective-permute-start.2
  73.6 28.3 %score_near.1 = (f32[1,1536]{1,0:T(1,128)S(1)}, bf16[1536,1024]{1,0:T(8,128)(2,1)S(1)}, bf16[3072,1024]{1,0:T(8,128)(2,1)S(1)}) custom-call(bf16[512,1024]{1,0:T(8,128)(2,1)} %get-tuple-element.15.refs_0_, bf16[512,1024]{1,0:T(8,128)(2,1)} %collective-permute-done.refs_1_, bf16[512,1024]{1,0:T(8,128)(2,1)} %collective-permute-done.4.refs_2_, ...), custom_call_target="tpu_custom_call" | custom-call | flops 1 | bytes 1 | tf_op jit(solution)/shard_map/score_near/pallas_call | solution.py:272
  101.9 0.0 copy-done
  101.9 0.0 copy-done.1
  101.9 0.9 pick.1
  102.8 0.0 collective-permute-done.5.refs_0_.refs_1_
  102.8 11.0 %score_mid.1 = f32[1,1536]{1,0:T(1,128)S(1)} custom-call(bf16[1024,1024]{1,0:T(8,128)(2,1)S(1)} %collective-permute-done.5.refs_0_.refs_1_, bf16[1536,1024]{1,0:T(8,128)(2,1)S(1)} %get-tuple-element.23.refs_1_, f32[1,1536]{1,0:T(1,128)S(1)} %get-tuple-element.24.refs_2_), custom_call_target="tpu_custom_call" | custom-call | flops 1 | bytes 1 | tf_op jit(solution)/shard_map/score_mid/pallas_call | solution.py:272
  113.9 0.0 collective-permute-done.2.refs_0_
  113.9 14.9 %score_far.1 = f32[1,512]{1,0:T(1,128)S(1)} custom-call(bf16[512,1024]{1,0:T(8,128)(2,1)S(1)} %collective-permute-done.2.refs_0_, bf16[1024,1024]{1,0:T(8,128)(2,1)S(1)} %collective-permute-done.5.refs_0_.refs_1_, bf16[3072,1024]{1,0:T(8,128)(2,1)S(1)} %get-tuple-element.27.refs_2_, f32[1,128]{1,0:T(1,128)S(1)} %broadcast_1_refs_3_.2.refs_3_), custom_call_target="tpu_custom_call" | custom-call | flops 1 | bytes 1 | tf_op jit(solution)/shard_map/score_far/pallas_call | solution.py:272
  128.8 1.4 collective-permute-start.6
  130.2 1.8 %collective-permute-start.7 = (f32[1,512]{1,0:T(1,128)S(1)}, f32[1,512]{1,0:T(1,128)S(1)}, u32[]{:S(2)}, u32[]{:S(2)}) collective-permute-start(f32[1,512]{1,0:T(1,128)S(1)} %get-tuple-element.30), channel_id=1, source_target_pairs={{0,12},{1,5},{4,0},{5,9},{8,4},{9,13},{12,8},{13,1},{2,14},{3,7},{... | collective-permute-start | bytes 6152 | tf_op jit(solution)/shard_map/ppermute | solution.py:398
  131.9 0.3 collective-permute-start.8
  132.2 1.8 %collective-permute-done.6 = f32[1,512]{1,0:T(1,128)S(1)} collective-permute-done((f32[1,512]{1,0:T(1,128)S(1)}, f32[1,512]{1,0:T(1,128)S(1)}, u32[]{:S(2)}, u32[]{:S(2)}) %collective-permute-start.6) | collective-permute-done | bytes 2080 | tf_op jit(solution)/shard_map/ppermute | solution.py:398
  134.0 0.0 collective-permute-done.7
  134.0 2.7 %collective-permute-done.8 = f32[1,512]{1,0:T(1,128)S(1)} collective-permute-done((f32[1,512]{1,0:T(1,128)S(1)}, f32[1,512]{1,0:T(1,128)S(1)}, u32[]{:S(2)}, u32[]{:S(2)}) %collective-permute-start.8) | collective-permute-done | bytes 2080 | tf_op jit(solution)/shard_map/ppermute | solution.py:398
  136.8 0.6 multiply_subtract_fusion
  (4 shorter events, 0.0 us)
Async XLA Ops:
  4.8 44.4 %all-to-all-start = ((bf16[128,8,1152]{2,1,0:T(8,128)(2,1)}), bf16[128,8,1152]{2,1,0:T(8,128)(2,1)S(1)}, u32[]{:S(2)}, u32[]{:S(2)}) async-start(bf16[128,8,1152]{2,1,0:T(8,128)(2,1)} %bitcast.16), calls=%async_computation | async-start | bytes 4718592 | tf_op jit(solution)/shard_map/all_to_all | solution.py:429
  15.9 4.5 %copy-start.3 = (bf16[512,1024]{1,0:T(8,128)(2,1)S(1)}, bf16[512,1024]{1,0:T(8,128)(2,1)}, u32[]{:S(2)}) copy-start(bf16[512,1024]{1,0:T(8,128)(2,1)} %get-tuple-element.15.refs_0_) | copy-start | bytes 3145732
  19.3 4.5 %collective-permute-start.1 = (bf16[1024,1024]{1,0:T(8,128)(2,1)}, bf16[1024,1024]{1,0:T(8,128)(2,1)S(1)}, u32[]{:S(2)}, u32[]{:S(2)}) collective-permute-start(bf16[1024,1024]{1,0:T(8,128)(2,1)} %prepare_centres.1.refs_1_.refs_4_), channel_id=1, source_target_pairs={{0,1},{1,0},{4,5},{5,4},{8,9},{9,8},{12,13},{13,12},{2,3},{3,2},{6... | collective-permute-start | bytes 6291464 | tf_op jit(solution)/shard_map/ppermute | solution.py:398
  19.4 47.3 %collective-permute-start.3 = (bf16[1024,1024]{1,0:T(8,128)(2,1)}, bf16[1024,1024]{1,0:T(8,128)(2,1)}, u32[]{:S(2)}, u32[]{:S(2)}) collective-permute-start(bf16[1024,1024]{1,0:T(8,128)(2,1)} %prepare_centres.1.refs_1_.refs_4_), channel_id=1, source_target_pairs={{0,2},{1,19},{4,6},{5,23},{8,10},{9,27},{12,14},{13,31},{2,16},{3,... | collective-permute-start | bytes 6291464 | tf_op jit(solution)/shard_map/ppermute | solution.py:398
  20.5 52.0 %collective-permute-start = (bf16[512,1024]{1,0:T(8,128)(2,1)S(1)}, bf16[512,1024]{1,0:T(8,128)(2,1)}, u32[]{:S(2)}, u32[]{:S(2)}) collective-permute-start(bf16[512,1024]{1,0:T(8,128)(2,1)S(1)} %copy-done.3), channel_id=1, source_target_pairs={{0,4},{1,13},{4,8},{5,1},{8,12},{9,5},{12,0},{13,9},{2,6},{3,15},{... | collective-permute-start | bytes 3145736 | tf_op jit(solution)/shard_map/ppermute | solution.py:398
  22.1 50.4 %collective-permute-start.4 = (bf16[512,1024]{1,0:T(8,128)(2,1)S(1)}, bf16[512,1024]{1,0:T(8,128)(2,1)}, u32[]{:S(2)}, u32[]{:S(2)}) collective-permute-start(bf16[512,1024]{1,0:T(8,128)(2,1)S(1)} %copy-done.3), channel_id=1, source_target_pairs={{0,12},{1,5},{4,0},{5,9},{8,4},{9,13},{12,8},{13,1},{2,14},{3,7},{... | collective-permute-start | bytes 3145736 | tf_op jit(solution)/shard_map/ppermute | solution.py:398
  23.8 1.4 %copy-start.2 = (bf16[1024,1024]{1,0:T(8,128)(2,1)}, bf16[1024,1024]{1,0:T(8,128)(2,1)S(1)}, u32[]{:S(2)}) copy-start(bf16[1024,1024]{1,0:T(8,128)(2,1)S(1)} %collective-permute-done.1.refs_2_.refs_5_) | copy-start | bytes 6291460
  52.6 19.9 %all-to-all-start.1 = ((f32[128,1,8]{2,1,0:T(1,128)}), f32[128,1,8]{2,1,0:T(1,128)S(1)}, u32[]{:S(2)}, u32[]{:S(2)}) async-start(f32[128,1,8]{2,1,0:T(1,128)} %bitcast.5), calls=%async_computation.1 | async-start | bytes 131072 | tf_op jit(solution)/shard_map/all_to_all | solution.py:437
  72.5 29.5 %copy-start = (s32[512]{0:T(512)S(1)}, s32[512]{0:T(512)}, u32[]{:S(2)}) copy-start(s32[512]{0:T(512)} %param.6) | copy-start | bytes 6148
  72.5 29.5 %copy-start.1 = (s32[512]{0:T(512)S(1)}, s32[512]{0:T(512)}, u32[]{:S(2)}) copy-start(s32[512]{0:T(512)} %param.7) | copy-start | bytes 6148
  72.5 30.3 %collective-permute-start.5 = (bf16[1024,1024]{1,0:T(8,128)(2,1)}, bf16[1024,1024]{1,0:T(8,128)(2,1)S(1)}, u32[]{:S(2)}, u32[]{:S(2)}) collective-permute-start(bf16[1024,1024]{1,0:T(8,128)(2,1)} %collective-permute-done.3.refs_3_), channel_id=1, source_target_pairs={{0,1},{1,0},{4,5},{5,4},{8,9},{9,8},{12,13},{13,12},{2,3},{3,2},{6... | collective-permute-start | bytes 6291464 | tf_op jit(solution)/shard_map/ppermute | solution.py:398
  72.6 41.3 %collective-permute-start.2 = (bf16[512,1024]{1,0:T(8,128)(2,1)}, bf16[512,1024]{1,0:T(8,128)(2,1)S(1)}, u32[]{:S(2)}, u32[]{:S(2)}) collective-permute-start(bf16[512,1024]{1,0:T(8,128)(2,1)} %collective-permute-done.refs_1_), channel_id=1, source_target_pairs={{0,4},{1,13},{4,8},{5,1},{8,12},{9,5},{12,0},{13,9},{2,6},{3,15},{... | collective-permute-start | bytes 3145736 | tf_op jit(solution)/shard_map/ppermute | solution.py:398
  128.8 5.2 %collective-permute-start.6 = (f32[1,512]{1,0:T(1,128)S(1)}, f32[1,512]{1,0:T(1,128)S(1)}, u32[]{:S(2)}, u32[]{:S(2)}) collective-permute-start(f32[1,512]{1,0:T(1,128)S(1)} %score_far.1), channel_id=1, source_target_pairs={{0,8},{1,9},{4,12},{5,13},{8,0},{9,1},{12,4},{13,5},{2,10},{3,11},... | collective-permute-start | bytes 6152 | tf_op jit(solution)/shard_map/ppermute | solution.py:398
  130.2 3.8 %collective-permute-start.7 = (f32[1,512]{1,0:T(1,128)S(1)}, f32[1,512]{1,0:T(1,128)S(1)}, u32[]{:S(2)}, u32[]{:S(2)}) collective-permute-start(f32[1,512]{1,0:T(1,128)S(1)} %get-tuple-element.30), channel_id=1, source_target_pairs={{0,12},{1,5},{4,0},{5,9},{8,4},{9,13},{12,8},{13,1},{2,14},{3,7},{... | collective-permute-start | bytes 6152 | tf_op jit(solution)/shard_map/ppermute | solution.py:398
  131.9 4.8 %collective-permute-start.8 = (f32[1,512]{1,0:T(1,128)S(1)}, f32[1,512]{1,0:T(1,128)S(1)}, u32[]{:S(2)}, u32[]{:S(2)}) collective-permute-start(f32[1,512]{1,0:T(1,128)S(1)} %get-tuple-element.31), channel_id=1, source_target_pairs={{0,4},{1,13},{4,8},{5,1},{8,12},{9,5},{12,0},{13,9},{2,6},{3,15},{... | collective-permute-start | bytes 6152 | tf_op jit(solution)/shard_map/ppermute | solution.py:398

commit v4 on v3

--- a/solution.py
+++ b/solution.py
@@ -23,6 +23,7 @@
 ANY = pl.BlockSpec(memory_space=pl.ANY)
 CHUNK = 128
 STEP = 512
+TILE = 1024
 
 
 def in_hbm(value):
@@ -194,7 +195,7 @@
         cents, cent_start, _ = cent_at[i]
         values, row_start, _ = row_at[j]
         return SCALE * lax.dot_general(
-            cents[pl.ds(cent_start + cent, STEP)],
+            cents[pl.ds(cent_start + cent, TILE)],
             values[pl.ds(row_start + row, LANES)],
             NT,
             preferred_element_type=jnp.float32,
@@ -225,12 +226,12 @@
         for i, j in products:
             for row in range(0, row_at[j][2], LANES):
                 lanes = slice(lane_at[j] + row, lane_at[j] + row + LANES)
-                for cent in range(0, cent_at[i][2], STEP):
+                for cent in range(0, cent_at[i][2], TILE):
                     value = product(i, j, cent, row)
                     if j not in begun and cent == 0:
                         shift = jnp.max(value, axis=0, keepdims=True)
                         high[:, lanes] = jnp.broadcast_to(shift, (8, LANES))
-                    value = jnp.exp2(value.reshape(STEP // 8, 8, LANES) - high[:, lanes][None])
+                    value = jnp.exp2(value.reshape(TILE // 8, 8, LANES) - high[:, lanes][None])
                     total[:, lanes] += jnp.sum(value, axis=0)
             begun.add(j)
 
@@ -241,11 +242,11 @@
 
             @pl.loop(0, row_at[j][2] // LANES)
             def _(r):
-                @pl.loop(0, cent_at[i][2] // STEP)
+                @pl.loop(0, cent_at[i][2] // TILE)
                 def _(c):
                     lanes = pl.ds(pl.multiple_of(lane_at[j] + r * LANES, LANES), LANES)
-                    row, cent = pl.multiple_of(r * LANES, LANES), pl.multiple_of(c * STEP, STEP)
-                    value = product(i, j, cent, row).reshape(STEP // 8, 8, LANES)
+                    row, cent = pl.multiple_of(r * LANES, LANES), pl.multiple_of(c * TILE, TILE)
+                    value = product(i, j, cent, row).reshape(TILE // 8, 8, LANES)
                     before = high[:, lanes]
                     now = jnp.maximum(before, jnp.max(value, axis=0))
                     high[:, lanes] = now
@@ -460,10 +461,10 @@
         (), (side_core,), plan, "score_mid", 16, prior=near, priors=(0, 1, 2), kept=(rows, sizes, None, ())
     )
     parts = [mid[:, i * row_count : (i + 1) * row_count] for i in range(3)]
-    dup_sim = pick(after(returned, near), cluster, slot, per_owner)
     plan = (((0,), (), ((1, 0), (2, 0), (3, 0))), ((), (0,), ((0, 0),)))
     kept = (None, (), table, (centre.shape[0],) * 3)
-    last = score((after(far, (mid, dup_sim)),), (side_core,), plan, "score_far", 16, kept=kept)
+    last = score((after(far, mid),), (side_core,), plan, "score_far", 16, kept=kept)
+    dup_sim = pick(after(returned, last), cluster, slot, per_owner)
     terms = (move_z(last, 2), parts[0], move_z(parts[1], -1), move_z(parts[2], 1))
     terms = jnp.concatenate(terms, axis=0)
     top = jnp.max(terms, axis=0)

time: 138 us -> 131 us (0.949)
  Pallas kernels: 75.7 us -> 69.1 us
    pallas_call x4, Pallas kernels: 64 us -> 57.4 us  [score(): pl.pallas_call(functools.partial(score_kernel, rows_new, rows_kept, cents...]
  transfers between devices with their start and end apart: 11 -> 11, of which waited for: 5 -> 5; matrix products, arithmetic and copies ran while one was open for 0% -> 0% of each run, Pallas kernels for 41% -> 40%
where the time goes in v4:
time: 131 us
  Pallas kernels  69.1 us (53%)
  waiting for transfers between devices  33.9 us (26%)
  starting transfers between devices  24.7 us (19%)
  local copies, waits for them, and re-layouts  1.41 us (1%)
    pallas_call x4, Pallas kernels, score(): pl.pallas_call(functools.partial(score_kernel, rows_new, rows_kept, cents...  57.4 us
    all_to_all x1, waiting for transfers between devices, per_device(): lax.all_to_all(send.reshape(devices, cap, width + ID_LANES), ('doc', 'cen...  15 us
    ppermute x9, waiting for transfers between devices, move(): return lax.ppermute(value, ('doc', 'cent'), pairs)  13.1 us
    all_to_all x1, starting transfers between devices, per_device(): lax.all_to_all(send.reshape(devices, cap, width + ID_LANES), ('doc', 'cen...  11.1 us
    ppermute x9, starting transfers between devices, move(): return lax.ppermute(value, ('doc', 'cent'), pairs)  8.94 us
    all_to_all x1, waiting for transfers between devices, per_device(): lax.all_to_all(best, ('doc', 'cent'), split_axis=0, concat_axis=0, tiled=...  5.81 us
    all_to_all x1, starting transfers between devices, per_device(): lax.all_to_all(best, ('doc', 'cent'), split_axis=0, concat_axis=0, tiled=...  4.62 us
    pallas_call x1, Pallas kernels, prepare_rows(): pl.pallas_call(functools.partial(rows_kernel, per_owner, cap), out_shape=...  4.14 us
  transfers between devices with their start and end apart: 11, of which 5 were waited for; matrix products, arithmetic and copies ran while one was open for 0% of the time, Pallas kernels for 40%

profile of v4, /device:TPU:0, one launch (start us, length us, event | category | flops | bytes accessed | tf_op | source)
XLA Modules:
  0.0 130.6 jit_solution(14702499590236672789)
XLA Ops:
  0.6 4.1 %prepare_rows.1 = (bf16[512,1024]{1,0:T(8,128)(2,1)}, bf16[1024,1152]{1,0:T(8,128)(2,1)}) custom-call(f32[512,1024]{1,0:T(8,128)} %refs_0_.1, s32[1,512]{1,0:T(1,128)} %bitcast.12, s32[1,512]{1,0:T(1,128)} %bitcast.14), custom_call_target="tpu_custom_call" | custom-call | flops 1 | bytes 1 | tf_op jit(solution)/shard_map/prepare_rows/pallas_call | solution.py:92
  4.8 11.1 %all-to-all-start = ((bf16[128,8,1152]{2,1,0:T(8,128)(2,1)}), bf16[128,8,1152]{2,1,0:T(8,128)(2,1)S(1)}, u32[]{:S(2)}, u32[]{:S(2)}) async-start(bf16[128,8,1152]{2,1,0:T(8,128)(2,1)} %bitcast.16), calls=%async_computation | async-start | bytes 4718592 | tf_op jit(solution)/shard_map/all_to_all | solution.py:430
  15.9 0.0 copy-start.3
  15.9 3.3 %prepare_centres.1.refs_1_.refs_4_ = bf16[1024,1024]{1,0:T(8,128)(2,1)} custom-call(f32[1024,1024]{1,0:T(8,128)} %cen_hbm), custom_call_target="tpu_custom_call" | custom-call | flops 1 | bytes 1 | tf_op jit(solution)/shard_map/prepare_centres/pallas_call | solution.py:133
  19.3 0.1 collective-permute-start.1
  19.4 1.1 collective-permute-start.3
  20.5 0.0 copy-done.3
  20.5 1.6 %collective-permute-start = (bf16[512,1024]{1,0:T(8,128)(2,1)S(1)}, bf16[512,1024]{1,0:T(8,128)(2,1)}, u32[]{:S(2)}, u32[]{:S(2)}) collective-permute-start(bf16[512,1024]{1,0:T(8,128)(2,1)S(1)} %copy-done.3), channel_id=1, source_target_pairs={{0,4},{1,13},{4,8},{5,1},{8,12},{9,5},{12,0},{13,9},{2,6},{3,15},{... | collective-permute-start | bytes 3145736 | tf_op jit(solution)/shard_map/ppermute | solution.py:399
  22.1 1.8 %collective-permute-start.4 = (bf16[512,1024]{1,0:T(8,128)(2,1)S(1)}, bf16[512,1024]{1,0:T(8,128)(2,1)}, u32[]{:S(2)}, u32[]{:S(2)}) collective-permute-start(bf16[512,1024]{1,0:T(8,128)(2,1)S(1)} %copy-done.3), channel_id=1, source_target_pairs={{0,12},{1,5},{4,0},{5,9},{8,4},{9,13},{12,8},{13,1},{2,14},{3,7},{... | collective-permute-start | bytes 3145736 | tf_op jit(solution)/shard_map/ppermute | solution.py:399
  23.8 0.0 collective-permute-done.1.refs_2_.refs_5_
  23.8 0.0 copy-start.2
  23.8 1.4 %copy-done.2 = bf16[1024,1024]{1,0:T(8,128)(2,1)} copy-done((bf16[1024,1024]{1,0:T(8,128)(2,1)}, bf16[1024,1024]{1,0:T(8,128)(2,1)S(1)}, u32[]{:S(2)}) %copy-start.2) | copy-done | bytes 2097176
  25.2 9.0 %score_own.1.refs_6_ = f32[1,512]{1,0:T(1,128)S(1)} custom-call(bf16[512,1024]{1,0:T(8,128)(2,1)} %get-tuple-element.15.refs_0_, bf16[1024,1024]{1,0:T(8,128)(2,1)} %prepare_centres.1.refs_1_.refs_4_, bf16[1024,1024]{1,0:T(8,128)(2,1)} %copy-done.2, f32[1,128]{1,0:T(1,128)S(1)} %broadcast_1_refs_3_.2.refs_3_), custom_call_target="tpu_custom_call" | custom-call | flops 1 | bytes 1 | tf_op jit(solution)/shard_map/score_own/pallas_call | solution.py:273
  34.2 15.0 %all-to-all-done = bf16[128,8,1152]{2,1,0:T(8,128)(2,1)S(1)} async-done(((bf16[128,8,1152]{2,1,0:T(8,128)(2,1)}), bf16[128,8,1152]{2,1,0:T(8,128)(2,1)S(1)}, u32[]{:S(2)}, u32[]{:S(2)}) %all-to-all-start) | async-done | bytes 2359328 | tf_op jit(solution)/shard_map/all_to_all | solution.py:430
  49.2 3.4 %owner_best.1 = f32[128,8]{1,0:T(8,128)} custom-call(bf16[1024,1152]{1,0:T(8,128)(2,1)S(1)} %bitcast.10), custom_call_target="tpu_custom_call" | custom-call | flops 1 | bytes 1 | tf_op jit(solution)/shard_map/owner_best/pallas_call | solution.py:343
  52.6 4.6 %all-to-all-start.1 = ((f32[128,1,8]{2,1,0:T(1,128)}), f32[128,1,8]{2,1,0:T(1,128)S(1)}, u32[]{:S(2)}, u32[]{:S(2)}) async-start(f32[128,1,8]{2,1,0:T(1,128)} %bitcast.5), calls=%async_computation.1 | async-start | bytes 131072 | tf_op jit(solution)/shard_map/all_to_all | solution.py:438
  57.2 9.4 %collective-permute-done.3.refs_3_ = bf16[1024,1024]{1,0:T(8,128)(2,1)} collective-permute-done((bf16[1024,1024]{1,0:T(8,128)(2,1)}, bf16[1024,1024]{1,0:T(8,128)(2,1)}, u32[]{:S(2)}, u32[]{:S(2)}) %collective-permute-start.3) | collective-permute-done | bytes 2097184 | tf_op jit(solution)/shard_map/ppermute | solution.py:399
  66.6 5.8 %all-to-all-done.1 = f32[128,1,8]{2,1,0:T(1,128)S(1)} async-done(((f32[128,1,8]{2,1,0:T(1,128)}), f32[128,1,8]{2,1,0:T(1,128)S(1)}, u32[]{:S(2)}, u32[]{:S(2)}) %all-to-all-start.1) | async-done | bytes 4128 | tf_op jit(solution)/shard_map/all_to_all | solution.py:438
  72.5 0.0 collective-permute-done.refs_1_
  72.5 0.0 collective-permute-done.4.refs_2_
  72.5 0.0 collective-permute-start.5
  72.5 1.1 collective-permute-start.2
  73.5 25.4 %score_near.1 = (f32[1,1536]{1,0:T(1,128)S(1)}, bf16[1536,1024]{1,0:T(8,128)(2,1)S(1)}, bf16[3072,1024]{1,0:T(8,128)(2,1)S(1)}) custom-call(bf16[512,1024]{1,0:T(8,128)(2,1)} %get-tuple-element.15.refs_0_, bf16[512,1024]{1,0:T(8,128)(2,1)} %collective-permute-done.refs_1_, bf16[512,1024]{1,0:T(8,128)(2,1)} %collective-permute-done.4.refs_2_, ...), custom_call_target="tpu_custom_call" | custom-call | flops 1 | bytes 1 | tf_op jit(solution)/shard_map/score_near/pallas_call | solution.py:273
  99.0 0.0 collective-permute-done.5.refs_0_.refs_1_
  99.0 9.7 %score_mid.1 = f32[1,1536]{1,0:T(1,128)S(1)} custom-call(bf16[1024,1024]{1,0:T(8,128)(2,1)S(1)} %collective-permute-done.5.refs_0_.refs_1_, bf16[1536,1024]{1,0:T(8,128)(2,1)S(1)} %get-tuple-element.23.refs_1_, f32[1,1536]{1,0:T(1,128)S(1)} %get-tuple-element.24.refs_2_), custom_call_target="tpu_custom_call" | custom-call | flops 1 | bytes 1 | tf_op jit(solution)/shard_map/score_mid/pallas_call | solution.py:273
  108.7 0.0 collective-permute-done.2.refs_0_
  108.7 0.0 copy-start
  108.7 0.0 copy-start.1
  108.8 13.3 %score_far.1 = f32[1,512]{1,0:T(1,128)S(1)} custom-call(bf16[512,1024]{1,0:T(8,128)(2,1)S(1)} %collective-permute-done.2.refs_0_, bf16[1024,1024]{1,0:T(8,128)(2,1)S(1)} %collective-permute-done.5.refs_0_.refs_1_, bf16[3072,1024]{1,0:T(8,128)(2,1)S(1)} %get-tuple-element.26.refs_2_, f32[1,128]{1,0:T(1,128)S(1)} %broadcast_1_refs_3_.2.refs_3_), custom_call_target="tpu_custom_call" | custom-call | flops 1 | bytes 1 | tf_op jit(solution)/shard_map/score_far/pallas_call | solution.py:273
  122.0 1.3 collective-permute-start.6
  123.3 1.8 %collective-permute-start.7 = (f32[1,512]{1,0:T(1,128)S(1)}, f32[1,512]{1,0:T(1,128)S(1)}, u32[]{:S(2)}, u32[]{:S(2)}) collective-permute-start(f32[1,512]{1,0:T(1,128)S(1)} %get-tuple-element.30), channel_id=1, source_target_pairs={{0,12},{1,5},{4,0},{5,9},{8,4},{9,13},{12,8},{13,1},{2,14},{3,7},{... | collective-permute-start | bytes 6152 | tf_op jit(solution)/shard_map/ppermute | solution.py:399
  125.1 0.2 collective-permute-start.8
  125.3 0.0 copy-done
  125.3 0.0 copy-done.1
  125.4 0.9 pick.1
  126.2 1.0 collective-permute-done.6
  127.2 0.0 collective-permute-done.7
  127.2 2.7 %collective-permute-done.8 = f32[1,512]{1,0:T(1,128)S(1)} collective-permute-done((f32[1,512]{1,0:T(1,128)S(1)}, f32[1,512]{1,0:T(1,128)S(1)}, u32[]{:S(2)}, u32[]{:S(2)}) %collective-permute-start.8) | collective-permute-done | bytes 2080 | tf_op jit(solution)/shard_map/ppermute | solution.py:399
  130.0 0.6 multiply_subtract_fusion
  (4 shorter events, 0.0 us)
Async XLA Ops:
  4.8 44.4 %all-to-all-start = ((bf16[128,8,1152]{2,1,0:T(8,128)(2,1)}), bf16[128,8,1152]{2,1,0:T(8,128)(2,1)S(1)}, u32[]{:S(2)}, u32[]{:S(2)}) async-start(bf16[128,8,1152]{2,1,0:T(8,128)(2,1)} %bitcast.16), calls=%async_computation | async-start | bytes 4718592 | tf_op jit(solution)/shard_map/all_to_all | solution.py:430
  15.9 4.5 %copy-start.3 = (bf16[512,1024]{1,0:T(8,128)(2,1)S(1)}, bf16[512,1024]{1,0:T(8,128)(2,1)}, u32[]{:S(2)}) copy-start(bf16[512,1024]{1,0:T(8,128)(2,1)} %get-tuple-element.15.refs_0_) | copy-start | bytes 3145732
  19.3 4.5 %collective-permute-start.1 = (bf16[1024,1024]{1,0:T(8,128)(2,1)}, bf16[1024,1024]{1,0:T(8,128)(2,1)S(1)}, u32[]{:S(2)}, u32[]{:S(2)}) collective-permute-start(bf16[1024,1024]{1,0:T(8,128)(2,1)} %prepare_centres.1.refs_1_.refs_4_), channel_id=1, source_target_pairs={{0,1},{1,0},{4,5},{5,4},{8,9},{9,8},{12,13},{13,12},{2,3},{3,2},{6... | collective-permute-start | bytes 6291464 | tf_op jit(solution)/shard_map/ppermute | solution.py:399
  19.4 47.3 %collective-permute-start.3 = (bf16[1024,1024]{1,0:T(8,128)(2,1)}, bf16[1024,1024]{1,0:T(8,128)(2,1)}, u32[]{:S(2)}, u32[]{:S(2)}) collective-permute-start(bf16[1024,1024]{1,0:T(8,128)(2,1)} %prepare_centres.1.refs_1_.refs_4_), channel_id=1, source_target_pairs={{0,2},{1,19},{4,6},{5,23},{8,10},{9,27},{12,14},{13,31},{2,16},{3,... | collective-permute-start | bytes 6291464 | tf_op jit(solution)/shard_map/ppermute | solution.py:399
  20.5 52.0 %collective-permute-start = (bf16[512,1024]{1,0:T(8,128)(2,1)S(1)}, bf16[512,1024]{1,0:T(8,128)(2,1)}, u32[]{:S(2)}, u32[]{:S(2)}) collective-permute-start(bf16[512,1024]{1,0:T(8,128)(2,1)S(1)} %copy-done.3), channel_id=1, source_target_pairs={{0,4},{1,13},{4,8},{5,1},{8,12},{9,5},{12,0},{13,9},{2,6},{3,15},{... | collective-permute-start | bytes 3145736 | tf_op jit(solution)/shard_map/ppermute | solution.py:399
  22.1 50.4 %collective-permute-start.4 = (bf16[512,1024]{1,0:T(8,128)(2,1)S(1)}, bf16[512,1024]{1,0:T(8,128)(2,1)}, u32[]{:S(2)}, u32[]{:S(2)}) collective-permute-start(bf16[512,1024]{1,0:T(8,128)(2,1)S(1)} %copy-done.3), channel_id=1, source_target_pairs={{0,12},{1,5},{4,0},{5,9},{8,4},{9,13},{12,8},{13,1},{2,14},{3,7},{... | collective-permute-start | bytes 3145736 | tf_op jit(solution)/shard_map/ppermute | solution.py:399
  23.8 1.4 %copy-start.2 = (bf16[1024,1024]{1,0:T(8,128)(2,1)}, bf16[1024,1024]{1,0:T(8,128)(2,1)S(1)}, u32[]{:S(2)}) copy-start(bf16[1024,1024]{1,0:T(8,128)(2,1)S(1)} %collective-permute-done.1.refs_2_.refs_5_) | copy-start | bytes 6291460
  52.6 19.9 %all-to-all-start.1 = ((f32[128,1,8]{2,1,0:T(1,128)}), f32[128,1,8]{2,1,0:T(1,128)S(1)}, u32[]{:S(2)}, u32[]{:S(2)}) async-start(f32[128,1,8]{2,1,0:T(1,128)} %bitcast.5), calls=%async_computation.1 | async-start | bytes 131072 | tf_op jit(solution)/shard_map/all_to_all | solution.py:438
  72.5 26.5 %collective-permute-start.5 = (bf16[1024,1024]{1,0:T(8,128)(2,1)}, bf16[1024,1024]{1,0:T(8,128)(2,1)S(1)}, u32[]{:S(2)}, u32[]{:S(2)}) collective-permute-start(bf16[1024,1024]{1,0:T(8,128)(2,1)} %collective-permute-done.3.refs_3_), channel_id=1, source_target_pairs={{0,1},{1,0},{4,5},{5,4},{8,9},{9,8},{12,13},{13,12},{2,3},{3,2},{6... | collective-permute-start | bytes 6291464 | tf_op jit(solution)/shard_map/ppermute | solution.py:399
  72.5 36.3 %collective-permute-start.2 = (bf16[512,1024]{1,0:T(8,128)(2,1)}, bf16[512,1024]{1,0:T(8,128)(2,1)S(1)}, u32[]{:S(2)}, u32[]{:S(2)}) collective-permute-start(bf16[512,1024]{1,0:T(8,128)(2,1)} %collective-permute-done.refs_1_), channel_id=1, source_target_pairs={{0,4},{1,13},{4,8},{5,1},{8,12},{9,5},{12,0},{13,9},{2,6},{3,15},{... | collective-permute-start | bytes 3145736 | tf_op jit(solution)/shard_map/ppermute | solution.py:399
  108.7 16.6 %copy-start = (s32[512]{0:T(512)S(1)}, s32[512]{0:T(512)}, u32[]{:S(2)}) copy-start(s32[512]{0:T(512)} %param.6) | copy-start | bytes 6148
  108.7 16.6 %copy-start.1 = (s32[512]{0:T(512)S(1)}, s32[512]{0:T(512)}, u32[]{:S(2)}) copy-start(s32[512]{0:T(512)} %param.7) | copy-start | bytes 6148
  122.0 5.2 %collective-permute-start.6 = (f32[1,512]{1,0:T(1,128)S(1)}, f32[1,512]{1,0:T(1,128)S(1)}, u32[]{:S(2)}, u32[]{:S(2)}) collective-permute-start(f32[1,512]{1,0:T(1,128)S(1)} %score_far.1), channel_id=1, source_target_pairs={{0,8},{1,9},{4,12},{5,13},{8,0},{9,1},{12,4},{13,5},{2,10},{3,11},... | collective-permute-start | bytes 6152 | tf_op jit(solution)/shard_map/ppermute | solution.py:399
  123.3 3.9 %collective-permute-start.7 = (f32[1,512]{1,0:T(1,128)S(1)}, f32[1,512]{1,0:T(1,128)S(1)}, u32[]{:S(2)}, u32[]{:S(2)}) collective-permute-start(f32[1,512]{1,0:T(1,128)S(1)} %get-tuple-element.30), channel_id=1, source_target_pairs={{0,12},{1,5},{4,0},{5,9},{8,4},{9,13},{12,8},{13,1},{2,14},{3,7},{... | collective-permute-start | bytes 6152 | tf_op jit(solution)/shard_map/ppermute | solution.py:399
  125.1 4.8 %collective-permute-start.8 = (f32[1,512]{1,0:T(1,128)S(1)}, f32[1,512]{1,0:T(1,128)S(1)}, u32[]{:S(2)}, u32[]{:S(2)}) collective-permute-start(f32[1,512]{1,0:T(1,128)S(1)} %get-tuple-element.31), channel_id=1, source_target_pairs={{0,4},{1,13},{4,8},{5,1},{8,12},{9,5},{12,0},{13,9},{2,6},{3,15},{... | collective-permute-start | bytes 6152 | tf_op jit(solution)/shard_map/ppermute | solution.py:399

commit v5 on v4

--- a/solution.py
+++ b/solution.py
@@ -21,7 +21,7 @@
 PARAMS = pltpu.CompilerParams(vmem_limit_bytes=60 * 1024 * 1024)
 SCORE_PARAMS = pltpu.CompilerParams(vmem_limit_bytes=24 * 1024 * 1024)
 ANY = pl.BlockSpec(memory_space=pl.ANY)
-CHUNK = 128
+CHUNK = 256
 STEP = 512
 TILE = 1024
 

time: 131 us -> 131 us (level)
  no operation moved by 1% of the time
where the time goes in v5:
time: 131 us; the launch traced here: 130 us
  Pallas kernels  69.1 us (53%)
  waiting for transfers between devices  33.8 us (26%)
  starting transfers between devices  24.8 us (19%)
  local copies, waits for them, and re-layouts  1.41 us (1%)
    pallas_call x4, Pallas kernels, score(): pl.pallas_call(functools.partial(score_kernel, rows_new, rows_kept, cents...  57.3 us
    all_to_all x1, waiting for transfers between devices, per_device(): lax.all_to_all(send.reshape(devices, cap, width + ID_LANES), ('doc', 'cen...  15 us
    ppermute x9, waiting for transfers between devices, move(): return lax.ppermute(value, ('doc', 'cent'), pairs)  13 us
    all_to_all x1, starting transfers between devices, per_device(): lax.all_to_all(send.reshape(devices, cap, width + ID_LANES), ('doc', 'cen...  11.1 us
    ppermute x9, starting transfers between devices, move(): return lax.ppermute(value, ('doc', 'cent'), pairs)  9.07 us
    all_to_all x1, waiting for transfers between devices, per_device(): lax.all_to_all(best, ('doc', 'cent'), split_axis=0, concat_axis=0, tiled=...  5.81 us
    all_to_all x1, starting transfers between devices, per_device(): lax.all_to_all(best, ('doc', 'cent'), split_axis=0, concat_axis=0, tiled=...  4.62 us
    pallas_call x1, Pallas kernels, prepare_rows(): pl.pallas_call(functools.partial(rows_kernel, per_owner, cap), out_shape=...  4.16 us
  transfers between devices with their start and end apart: 11, of which 5 were waited for; matrix products, arithmetic and copies ran while one was open for 0% of the time, Pallas kernels for 40%

profile of v5, /device:TPU:0, one launch (start us, length us, event | category | flops | bytes accessed | tf_op | source)
XLA Modules:
  0.0 130.5 jit_solution(11325911076234548367)
XLA Ops:
  0.6 4.2 %prepare_rows.1 = (bf16[512,1024]{1,0:T(8,128)(2,1)}, bf16[1024,1152]{1,0:T(8,128)(2,1)}) custom-call(f32[512,1024]{1,0:T(8,128)} %refs_0_.1, s32[1,512]{1,0:T(1,128)} %bitcast.12, s32[1,512]{1,0:T(1,128)} %bitcast.14), custom_call_target="tpu_custom_call" | custom-call | flops 1 | bytes 1 | tf_op jit(solution)/shard_map/prepare_rows/pallas_call | solution.py:92
  4.8 11.1 %all-to-all-start = ((bf16[128,8,1152]{2,1,0:T(8,128)(2,1)}), bf16[128,8,1152]{2,1,0:T(8,128)(2,1)S(1)}, u32[]{:S(2)}, u32[]{:S(2)}) async-start(bf16[128,8,1152]{2,1,0:T(8,128)(2,1)} %bitcast.16), calls=%async_computation | async-start | bytes 4718592 | tf_op jit(solution)/shard_map/all_to_all | solution.py:430
  16.0 0.0 copy-start.3
  16.0 3.3 %prepare_centres.1.refs_1_.refs_4_ = bf16[1024,1024]{1,0:T(8,128)(2,1)} custom-call(f32[1024,1024]{1,0:T(8,128)} %cen_hbm), custom_call_target="tpu_custom_call" | custom-call | flops 1 | bytes 1 | tf_op jit(solution)/shard_map/prepare_centres/pallas_call | solution.py:133
  19.3 0.1 collective-permute-start.1
  19.4 1.1 collective-permute-start.3
  20.5 0.0 copy-done.3
  20.5 1.6 %collective-permute-start = (bf16[512,1024]{1,0:T(8,128)(2,1)S(1)}, bf16[512,1024]{1,0:T(8,128)(2,1)}, u32[]{:S(2)}, u32[]{:S(2)}) collective-permute-start(bf16[512,1024]{1,0:T(8,128)(2,1)S(1)} %copy-done.3), channel_id=1, source_target_pairs={{0,4},{1,13},{4,8},{5,1},{8,12},{9,5},{12,0},{13,9},{2,6},{3,15},{... | collective-permute-start | bytes 3145736 | tf_op jit(solution)/shard_map/ppermute | solution.py:399
  22.1 1.8 %collective-permute-start.4 = (bf16[512,1024]{1,0:T(8,128)(2,1)S(1)}, bf16[512,1024]{1,0:T(8,128)(2,1)}, u32[]{:S(2)}, u32[]{:S(2)}) collective-permute-start(bf16[512,1024]{1,0:T(8,128)(2,1)S(1)} %copy-done.3), channel_id=1, source_target_pairs={{0,12},{1,5},{4,0},{5,9},{8,4},{9,13},{12,8},{13,1},{2,14},{3,7},{... | collective-permute-start | bytes 3145736 | tf_op jit(solution)/shard_map/ppermute | solution.py:399
  23.8 0.0 collective-permute-done.1.refs_2_.refs_5_
  23.8 0.0 copy-start.2
  23.8 1.4 %copy-done.2 = bf16[1024,1024]{1,0:T(8,128)(2,1)} copy-done((bf16[1024,1024]{1,0:T(8,128)(2,1)}, bf16[1024,1024]{1,0:T(8,128)(2,1)S(1)}, u32[]{:S(2)}) %copy-start.2) | copy-done | bytes 2097176
  25.2 9.0 %score_own.1.refs_6_ = f32[1,512]{1,0:T(1,128)S(1)} custom-call(bf16[512,1024]{1,0:T(8,128)(2,1)} %get-tuple-element.15.refs_0_, bf16[1024,1024]{1,0:T(8,128)(2,1)} %prepare_centres.1.refs_1_.refs_4_, bf16[1024,1024]{1,0:T(8,128)(2,1)} %copy-done.2, f32[1,128]{1,0:T(1,128)S(1)} %broadcast_1_refs_3_.2.refs_3_), custom_call_target="tpu_custom_call" | custom-call | flops 1 | bytes 1 | tf_op jit(solution)/shard_map/score_own/pallas_call | solution.py:273
  34.2 15.0 %all-to-all-done = bf16[128,8,1152]{2,1,0:T(8,128)(2,1)S(1)} async-done(((bf16[128,8,1152]{2,1,0:T(8,128)(2,1)}), bf16[128,8,1152]{2,1,0:T(8,128)(2,1)S(1)}, u32[]{:S(2)}, u32[]{:S(2)}) %all-to-all-start) | async-done | bytes 2359328 | tf_op jit(solution)/shard_map/all_to_all | solution.py:430
  49.2 3.4 %owner_best.1 = f32[128,8]{1,0:T(8,128)} custom-call(bf16[1024,1152]{1,0:T(8,128)(2,1)S(1)} %bitcast.10), custom_call_target="tpu_custom_call" | custom-call | flops 1 | bytes 1 | tf_op jit(solution)/shard_map/owner_best/pallas_call | solution.py:343
  52.6 4.6 %all-to-all-start.1 = ((f32[128,1,8]{2,1,0:T(1,128)}), f32[128,1,8]{2,1,0:T(1,128)S(1)}, u32[]{:S(2)}, u32[]{:S(2)}) async-start(f32[128,1,8]{2,1,0:T(1,128)} %bitcast.5), calls=%async_computation.1 | async-start | bytes 131072 | tf_op jit(solution)/shard_map/all_to_all | solution.py:438
  57.2 9.4 %collective-permute-done.3.refs_3_ = bf16[1024,1024]{1,0:T(8,128)(2,1)} collective-permute-done((bf16[1024,1024]{1,0:T(8,128)(2,1)}, bf16[1024,1024]{1,0:T(8,128)(2,1)}, u32[]{:S(2)}, u32[]{:S(2)}) %collective-permute-start.3) | collective-permute-done | bytes 2097184 | tf_op jit(solution)/shard_map/ppermute | solution.py:399
  66.7 5.8 %all-to-all-done.1 = f32[128,1,8]{2,1,0:T(1,128)S(1)} async-done(((f32[128,1,8]{2,1,0:T(1,128)}), f32[128,1,8]{2,1,0:T(1,128)S(1)}, u32[]{:S(2)}, u32[]{:S(2)}) %all-to-all-start.1) | async-done | bytes 4128 | tf_op jit(solution)/shard_map/all_to_all | solution.py:438
  72.5 0.0 collective-permute-done.refs_1_
  72.5 0.0 collective-permute-done.4.refs_2_
  72.5 0.0 collective-permute-start.5
  72.5 1.1 collective-permute-start.2
  73.6 25.3 %score_near.1 = (f32[1,1536]{1,0:T(1,128)S(1)}, bf16[1536,1024]{1,0:T(8,128)(2,1)S(1)}, bf16[3072,1024]{1,0:T(8,128)(2,1)S(1)}) custom-call(bf16[512,1024]{1,0:T(8,128)(2,1)} %get-tuple-element.15.refs_0_, bf16[512,1024]{1,0:T(8,128)(2,1)} %collective-permute-done.refs_1_, bf16[512,1024]{1,0:T(8,128)(2,1)} %collective-permute-done.4.refs_2_, ...), custom_call_target="tpu_custom_call" | custom-call | flops 1 | bytes 1 | tf_op jit(solution)/shard_map/score_near/pallas_call | solution.py:273
  98.9 0.0 collective-permute-done.5.refs_0_.refs_1_
  98.9 9.7 %score_mid.1 = f32[1,1536]{1,0:T(1,128)S(1)} custom-call(bf16[1024,1024]{1,0:T(8,128)(2,1)S(1)} %collective-permute-done.5.refs_0_.refs_1_, bf16[1536,1024]{1,0:T(8,128)(2,1)S(1)} %get-tuple-element.23.refs_1_, f32[1,1536]{1,0:T(1,128)S(1)} %get-tuple-element.24.refs_2_), custom_call_target="tpu_custom_call" | custom-call | flops 1 | bytes 1 | tf_op jit(solution)/shard_map/score_mid/pallas_call | solution.py:273
  108.7 0.0 collective-permute-done.2.refs_0_
  108.7 0.0 copy-start
  108.7 0.0 copy-start.1
  108.7 13.3 %score_far.1 = f32[1,512]{1,0:T(1,128)S(1)} custom-call(bf16[512,1024]{1,0:T(8,128)(2,1)S(1)} %collective-permute-done.2.refs_0_, bf16[1024,1024]{1,0:T(8,128)(2,1)S(1)} %collective-permute-done.5.refs_0_.refs_1_, bf16[3072,1024]{1,0:T(8,128)(2,1)S(1)} %get-tuple-element.26.refs_2_, f32[1,128]{1,0:T(1,128)S(1)} %broadcast_1_refs_3_.2.refs_3_), custom_call_target="tpu_custom_call" | custom-call | flops 1 | bytes 1 | tf_op jit(solution)/shard_map/score_far/pallas_call | solution.py:273
  122.0 1.4 %collective-permute-start.6 = (f32[1,512]{1,0:T(1,128)S(1)}, f32[1,512]{1,0:T(1,128)S(1)}, u32[]{:S(2)}, u32[]{:S(2)}) collective-permute-start(f32[1,512]{1,0:T(1,128)S(1)} %score_far.1), channel_id=1, source_target_pairs={{0,8},{1,9},{4,12},{5,13},{8,0},{9,1},{12,4},{13,5},{2,10},{3,11},... | collective-permute-start | bytes 6152 | tf_op jit(solution)/shard_map/ppermute | solution.py:399
  123.4 1.7 %collective-permute-start.7 = (f32[1,512]{1,0:T(1,128)S(1)}, f32[1,512]{1,0:T(1,128)S(1)}, u32[]{:S(2)}, u32[]{:S(2)}) collective-permute-start(f32[1,512]{1,0:T(1,128)S(1)} %get-tuple-element.30), channel_id=1, source_target_pairs={{0,12},{1,5},{4,0},{5,9},{8,4},{9,13},{12,8},{13,1},{2,14},{3,7},{... | collective-permute-start | bytes 6152 | tf_op jit(solution)/shard_map/ppermute | solution.py:399
  125.1 0.4 collective-permute-start.8
  125.4 0.0 copy-done
  125.4 0.0 copy-done.1
  125.4 0.9 pick.1
  126.3 0.8 collective-permute-done.6
  127.1 0.0 collective-permute-done.7
  127.1 2.7 %collective-permute-done.8 = f32[1,512]{1,0:T(1,128)S(1)} collective-permute-done((f32[1,512]{1,0:T(1,128)S(1)}, f32[1,512]{1,0:T(1,128)S(1)}, u32[]{:S(2)}, u32[]{:S(2)}) %collective-permute-start.8) | collective-permute-done | bytes 2080 | tf_op jit(solution)/shard_map/ppermute | solution.py:399
  129.9 0.6 multiply_subtract_fusion
  (4 shorter events, 0.0 us)
Async XLA Ops:
  4.8 44.4 %all-to-all-start = ((bf16[128,8,1152]{2,1,0:T(8,128)(2,1)}), bf16[128,8,1152]{2,1,0:T(8,128)(2,1)S(1)}, u32[]{:S(2)}, u32[]{:S(2)}) async-start(bf16[128,8,1152]{2,1,0:T(8,128)(2,1)} %bitcast.16), calls=%async_computation | async-start | bytes 4718592 | tf_op jit(solution)/shard_map/all_to_all | solution.py:430
  16.0 4.5 %copy-start.3 = (bf16[512,1024]{1,0:T(8,128)(2,1)S(1)}, bf16[512,1024]{1,0:T(8,128)(2,1)}, u32[]{:S(2)}) copy-start(bf16[512,1024]{1,0:T(8,128)(2,1)} %get-tuple-element.15.refs_0_) | copy-start | bytes 3145732
  19.3 4.5 %collective-permute-start.1 = (bf16[1024,1024]{1,0:T(8,128)(2,1)}, bf16[1024,1024]{1,0:T(8,128)(2,1)S(1)}, u32[]{:S(2)}, u32[]{:S(2)}) collective-permute-start(bf16[1024,1024]{1,0:T(8,128)(2,1)} %prepare_centres.1.refs_1_.refs_4_), channel_id=1, source_target_pairs={{0,1},{1,0},{4,5},{5,4},{8,9},{9,8},{12,13},{13,12},{2,3},{3,2},{6... | collective-permute-start | bytes 6291464 | tf_op jit(solution)/shard_map/ppermute | solution.py:399
  19.4 47.3 %collective-permute-start.3 = (bf16[1024,1024]{1,0:T(8,128)(2,1)}, bf16[1024,1024]{1,0:T(8,128)(2,1)}, u32[]{:S(2)}, u32[]{:S(2)}) collective-permute-start(bf16[1024,1024]{1,0:T(8,128)(2,1)} %prepare_centres.1.refs_1_.refs_4_), channel_id=1, source_target_pairs={{0,2},{1,19},{4,6},{5,23},{8,10},{9,27},{12,14},{13,31},{2,16},{3,... | collective-permute-start | bytes 6291464 | tf_op jit(solution)/shard_map/ppermute | solution.py:399
  20.5 52.0 %collective-permute-start = (bf16[512,1024]{1,0:T(8,128)(2,1)S(1)}, bf16[512,1024]{1,0:T(8,128)(2,1)}, u32[]{:S(2)}, u32[]{:S(2)}) collective-permute-start(bf16[512,1024]{1,0:T(8,128)(2,1)S(1)} %copy-done.3), channel_id=1, source_target_pairs={{0,4},{1,13},{4,8},{5,1},{8,12},{9,5},{12,0},{13,9},{2,6},{3,15},{... | collective-permute-start | bytes 3145736 | tf_op jit(solution)/shard_map/ppermute | solution.py:399
  22.1 50.4 %collective-permute-start.4 = (bf16[512,1024]{1,0:T(8,128)(2,1)S(1)}, bf16[512,1024]{1,0:T(8,128)(2,1)}, u32[]{:S(2)}, u32[]{:S(2)}) collective-permute-start(bf16[512,1024]{1,0:T(8,128)(2,1)S(1)} %copy-done.3), channel_id=1, source_target_pairs={{0,12},{1,5},{4,0},{5,9},{8,4},{9,13},{12,8},{13,1},{2,14},{3,7},{... | collective-permute-start | bytes 3145736 | tf_op jit(solution)/shard_map/ppermute | solution.py:399
  23.8 1.4 %copy-start.2 = (bf16[1024,1024]{1,0:T(8,128)(2,1)}, bf16[1024,1024]{1,0:T(8,128)(2,1)S(1)}, u32[]{:S(2)}) copy-start(bf16[1024,1024]{1,0:T(8,128)(2,1)S(1)} %collective-permute-done.1.refs_2_.refs_5_) | copy-start | bytes 6291460
  52.6 19.9 %all-to-all-start.1 = ((f32[128,1,8]{2,1,0:T(1,128)}), f32[128,1,8]{2,1,0:T(1,128)S(1)}, u32[]{:S(2)}, u32[]{:S(2)}) async-start(f32[128,1,8]{2,1,0:T(1,128)} %bitcast.5), calls=%async_computation.1 | async-start | bytes 131072 | tf_op jit(solution)/shard_map/all_to_all | solution.py:438
  72.5 26.4 %collective-permute-start.5 = (bf16[1024,1024]{1,0:T(8,128)(2,1)}, bf16[1024,1024]{1,0:T(8,128)(2,1)S(1)}, u32[]{:S(2)}, u32[]{:S(2)}) collective-permute-start(bf16[1024,1024]{1,0:T(8,128)(2,1)} %collective-permute-done.3.refs_3_), channel_id=1, source_target_pairs={{0,1},{1,0},{4,5},{5,4},{8,9},{9,8},{12,13},{13,12},{2,3},{3,2},{6... | collective-permute-start | bytes 6291464 | tf_op jit(solution)/shard_map/ppermute | solution.py:399
  72.5 36.2 %collective-permute-start.2 = (bf16[512,1024]{1,0:T(8,128)(2,1)}, bf16[512,1024]{1,0:T(8,128)(2,1)S(1)}, u32[]{:S(2)}, u32[]{:S(2)}) collective-permute-start(bf16[512,1024]{1,0:T(8,128)(2,1)} %collective-permute-done.refs_1_), channel_id=1, source_target_pairs={{0,4},{1,13},{4,8},{5,1},{8,12},{9,5},{12,0},{13,9},{2,6},{3,15},{... | collective-permute-start | bytes 3145736 | tf_op jit(solution)/shard_map/ppermute | solution.py:399
  108.7 16.7 %copy-start = (s32[512]{0:T(512)S(1)}, s32[512]{0:T(512)}, u32[]{:S(2)}) copy-start(s32[512]{0:T(512)} %param.6) | copy-start | bytes 6148
  108.7 16.7 %copy-start.1 = (s32[512]{0:T(512)S(1)}, s32[512]{0:T(512)}, u32[]{:S(2)}) copy-start(s32[512]{0:T(512)} %param.7) | copy-start | bytes 6148
  122.0 5.2 %collective-permute-start.6 = (f32[1,512]{1,0:T(1,128)S(1)}, f32[1,512]{1,0:T(1,128)S(1)}, u32[]{:S(2)}, u32[]{:S(2)}) collective-permute-start(f32[1,512]{1,0:T(1,128)S(1)} %score_far.1), channel_id=1, source_target_pairs={{0,8},{1,9},{4,12},{5,13},{8,0},{9,1},{12,4},{13,5},{2,10},{3,11},... | collective-permute-start | bytes 6152 | tf_op jit(solution)/shard_map/ppermute | solution.py:399
  123.4 3.7 %collective-permute-start.7 = (f32[1,512]{1,0:T(1,128)S(1)}, f32[1,512]{1,0:T(1,128)S(1)}, u32[]{:S(2)}, u32[]{:S(2)}) collective-permute-start(f32[1,512]{1,0:T(1,128)S(1)} %get-tuple-element.30), channel_id=1, source_target_pairs={{0,12},{1,5},{4,0},{5,9},{8,4},{9,13},{12,8},{13,1},{2,14},{3,7},{... | collective-permute-start | bytes 6152 | tf_op jit(solution)/shard_map/ppermute | solution.py:399
  125.1 4.8 %collective-permute-start.8 = (f32[1,512]{1,0:T(1,128)S(1)}, f32[1,512]{1,0:T(1,128)S(1)}, u32[]{:S(2)}, u32[]{:S(2)}) collective-permute-start(f32[1,512]{1,0:T(1,128)S(1)} %get-tuple-element.31), channel_id=1, source_target_pairs={{0,4},{1,13},{4,8},{5,1},{8,12},{9,5},{12,0},{13,9},{2,6},{3,15},{... | collective-permute-start | bytes 6152 | tf_op jit(solution)/shard_map/ppermute | solution.py:399
